TPU v7x, 512 devices: a whole 4x8x8 slice. The times are simulated.
512 devices in a mesh: outer: 8 (over z_lo, core), dev: 64 (over x, z_hi, y).
Axes of the slice: x: 4, y: 8, z: 8 (z_hi: 2, z_lo: 4; z = z_hi * 4 + z_lo), core: 2. Of those that a mesh axis runs over, the one named last changes fastest.
Arguments:
- pseudo_grad: float32 [8, 8192, 256], P('outer', 'dev'), may hold values from -6 to 6
- grad_expo: int32 [8, 8192], P('outer', 'dev'), may hold values from -2 to 2
- sign_bits: int32 [8192, 256], P('dev'), may hold values from 0 to 1
- params: float32 [8192, 256], P(('dev', 'outer')), may hold values from -6 to 6
- momentum: float32 [8192, 256], P(('dev', 'outer')), may hold values from -6 to 6
- param_expo: int32 [8192], P(('dev', 'outer')), may hold values from -2 to 2
Outputs:
- new_params: float32 [8192, 256], P(('dev', 'outer'))
- new_momentum: float32 [8192, 256], P(('dev', 'outer'))
- fragment_codes: bfloat16 [8192, 256], replicated
Inputs may be any that keep to these rules, and one draw needn't show every extreme that they name: `sign_bits`: 0 stands for the sign -1 and 1 for +1.
All inputs are finite; a program needn't handle non-finite values.
Results may differ from a plain program's by a relative error of at most 0.0085.
Values may be sent and summed in bfloat16 or wider, within the bound.
No kernel may reach another device: no remote copies, remote signals or barrier semaphores. Data moves between devices by JAX's collectives and lax.ppermute only.
A program may use at most 64 MiB of HBM per device.

v0:
```python
import jax
import jax.numpy as jnp
from jax import lax
from jax.sharding import PartitionSpec as P


def hadamard(width):
    index = jnp.arange(width, dtype=jnp.int32)
    common = index[:, None] & index[None, :]
    parity = jnp.zeros((width, width), jnp.int32)
    for bit in range(width.bit_length() - 1):
        parity = parity + (common >> bit & 1)
    return (1 - 2 * (parity % 2)).astype(jnp.float32)


def per_device(pseudo_grad, grad_expo, sign_bits, params, momentum, param_expo):
    width = sign_bits.shape[1]
    owned = params.shape[0]
    replicas = lax.axis_size("outer")
    table = hadamard(width)
    inv_root = 1.0 / jnp.sqrt(jnp.float32(width))
    sign = (2 * sign_bits - 1).astype(jnp.float32)
    rotated = jnp.dot(pseudo_grad[0] * sign, table, precision=lax.Precision.HIGHEST) * inv_root
    expo_float = grad_expo[0].astype(jnp.float32)
    grad_code = jnp.clip(rotated / jnp.exp2(expo_float)[:, None], -4.0, 4.0).astype(jnp.bfloat16)
    codes_in, expo_in = (
        lax.all_to_all(grad_code, "outer", split_axis=0, concat_axis=0, tiled=True),
        lax.all_to_all(
            expo_float.astype(jnp.bfloat16), "outer", split_axis=0, concat_axis=0, tiled=True
        ),
    )
    scaled = codes_in.astype(jnp.float32) * jnp.exp2(expo_in.astype(jnp.float32))[:, None]
    spread = jnp.dot(scaled, table, precision=lax.Precision.HIGHEST) * inv_root
    start = lax.axis_index("outer") * owned
    own_sign = lax.dynamic_slice_in_dim(sign, start, owned, 0)
    total = jnp.sum(spread.reshape(replicas, owned, width), axis=0) * own_sign
    delta = total / replicas
    new_momentum = 0.9 * momentum + delta
    new_params = params - 0.7 * (delta + 0.9 * new_momentum)
    param_scale = jnp.exp2(param_expo.astype(jnp.float32))
    own_codes = jnp.clip(new_params / param_scale[:, None], -4.0, 4.0).astype(jnp.bfloat16)
    shard_codes = lax.all_gather(own_codes, "outer", axis=0, tiled=True)
    fragment_codes = lax.all_gather(shard_codes, "dev", axis=0, tiled=True)
    return (new_params, new_momentum, fragment_codes)


def solution(mesh):
    in_specs = (
        P("outer", "dev", None),
        P("outer", "dev"),
        P("dev", None),
        P(("dev", "outer"), None),
        P(("dev", "outer"), None),
        P(("dev", "outer")),
    )
    out_specs = (P(("dev", "outer"), None), P(("dev", "outer"), None), P())
    return jax.shard_map(
        per_device, mesh=mesh, in_specs=in_specs, out_specs=out_specs, check_vma=False
    )
```

profile of v0, /device:TPU:1, one launch (start us, length us, event | category | flops | bytes accessed | tf_op | source)
XLA Modules:
  0.0 216.4 jit_solution(4461791266344886527)
XLA Ops:
  7.2 0.0 copy-start.1
  7.2 0.0 copy-start
  7.2 0.7 convert_reduce_fusion
  7.9 0.7 convert_element_type.72
  8.6 10.1 %all-to-all-start.1 = ((bf16[8,16,1]{1,2,0:T(2,128)(2,1)}), bf16[8,16,1]{1,2,0:T(2,128)(2,1)S(1)}, u32[]{:S(2)}, u32[]{:S(2)}) async-start(bf16[8,16,1]{1,2,0:T(2,128)(2,1)} %convert_element_type.72), calls=%async_computation.1 | async-start | bytes 8192 | tf_op jit(solution)/shard_map/all_to_all | solution.py:28
  18.6 0.7 exponential_bitcast_fusion
  19.3 2.2 %fusion.2 = bf16[128,256]{1,0:T(8,128)(2,1)} fusion(f32[1,128,256]{2,1,0:T(8,128)} %param.6, f32[128]{0:T(128)S(1)} %exponential_bitcast_fusion, s32[128,256]{1,0:T(8,128)} %param.8), kind=kOutput, calls=%fused_computation.4 | convolution fusion | flops 103415808 | bytes 328192 | tf_op jit(solution)/shard_map/dot_general | solution.py:23
  21.5 0.9 add_convert_fusion
  22.5 1.0 all-to-all-done.1
  23.5 4.1 %all-to-all-start = ((bf16[8,16,256]{2,1,0:T(8,128)(2,1)}), bf16[8,16,256]{2,1,0:T(8,128)(2,1)S(1)}, u32[]{:S(2)}, u32[]{:S(2)}) async-start(bf16[8,16,256]{2,1,0:T(8,128)(2,1)} %bitcast.2), calls=%async_computation | async-start | bytes 131072 | tf_op jit(solution)/shard_map/all_to_all | solution.py:27
  27.6 0.0 all-gather.2.cloned.1.call-start
  27.6 0.7 multiply_exponential_fusion
  28.3 0.1 exp2.47
  28.4 4.3 %all-to-all-done = bf16[8,16,256]{2,1,0:T(8,128)(2,1)S(1)} async-done(((bf16[8,16,256]{2,1,0:T(8,128)(2,1)}), bf16[8,16,256]{2,1,0:T(8,128)(2,1)S(1)}, u32[]{:S(2)}, u32[]{:S(2)}) %all-to-all-start) | async-done | bytes 65568 | tf_op jit(solution)/shard_map/all_to_all | solution.py:27
  32.7 0.6 convolution_multiply_fusion
  33.3 0.0 copy-done.1
  33.3 0.0 copy-done
  33.3 0.6 clamp_convert_fusion
  34.0 15.7 %all_gather.6 = bf16[128,256]{1,0:T(8,128)(2,1)} all-gather(bf16[16,256]{1,0:T(8,128)(2,1)S(1)} %get-tuple-element.3), channel_id=1, replica_groups=mesh['outer'=8,'dev'=64] {'outer'}, dimensions={0}, use_global_device_ids=true | all-gather | bytes 73728 | tf_op jit(solution)/shard_map/all_gather | solution.py:42
  49.7 0.0 all-gather.2.cloned.1.call-update
  49.7 155.4 %all-gather.2.cloned.1.call-done = bf16[8192,256]{1,0:T(8,128)(2,1)} async-done(((bf16[128,256]{1,0:T(8,128)(2,1)}), bf16[8192,256]{1,0:T(8,128)(2,1)}) %all-gather.2.cloned.1.call-update) | async-done | bytes 4194320 | tf_op jit(solution)/shard_map/all_gather | solution.py:43
  205.0 4.5 %copy.11 = bf16[8192,256]{1,0:T(8,128)(2,1)} copy(bf16[8192,256]{1,0:T(8,128)(2,1)} %all-gather.2.cloned.1.call-done) | data formatting | bytes 8388608
  (2 shorter events, 0.0 us)
Async XLA Ops:
  7.2 26.2 %copy-start.1 = (f32[16,256]{1,0:T(8,128)S(1)}, f32[16,256]{1,0:T(8,128)}, u32[]{:S(2)}) copy-start(f32[16,256]{1,0:T(8,128)} %param.10) | copy-start | bytes 49156
  7.2 26.2 %copy-start = (f32[16,256]{1,0:T(8,128)S(1)}, f32[16,256]{1,0:T(8,128)}, u32[]{:S(2)}) copy-start(f32[16,256]{1,0:T(8,128)} %param.9) | copy-start | bytes 49156
  8.6 14.9 %all-to-all-start.1 = ((bf16[8,16,1]{1,2,0:T(2,128)(2,1)}), bf16[8,16,1]{1,2,0:T(2,128)(2,1)S(1)}, u32[]{:S(2)}, u32[]{:S(2)}) async-start(bf16[8,16,1]{1,2,0:T(2,128)(2,1)} %convert_element_type.72), calls=%async_computation.1 | async-start | bytes 8192 | tf_op jit(solution)/shard_map/all_to_all | solution.py:28
  23.5 9.2 %all-to-all-start = ((bf16[8,16,256]{2,1,0:T(8,128)(2,1)}), bf16[8,16,256]{2,1,0:T(8,128)(2,1)S(1)}, u32[]{:S(2)}, u32[]{:S(2)}) async-start(bf16[8,16,256]{2,1,0:T(8,128)(2,1)} %bitcast.2), calls=%async_computation | async-start | bytes 131072 | tf_op jit(solution)/shard_map/all_to_all | solution.py:27
  27.6 177.4 %all-gather.2.cloned.1.call-start = ((), (), s32[]{:S(2)}) async-start(), calls=%async_computation.2 | async-start | bytes 4259840 | tf_op jit(solution)/shard_map/all_gather | solution.py:43
Sparse Core Ops, SparseCore 0:
  49.8 155.1 all-gather.1
where the time goes:
time: 219 us; the launch traced here: 216 us
  waiting for transfers between devices  161 us (74%)
  blocking collectives  15.7 us (7%)
  starting transfers between devices  14.2 us (6%)
  between operations  14.1 us (6%)
  local copies, waits for them, and re-layouts  5.24 us (2%)
  other arithmetic  3.59 us (2%)
  matrix products  2.83 us (1%)
    all_gather x1, waiting for transfers between devices, per_device(): fragment_codes = lax.all_gather(shard_codes, 'dev', axis=0, tiled=True)  155 us
    all_gather x1, blocking collectives, per_device(): shard_codes = lax.all_gather(own_codes, 'outer', axis=0, tiled=True)  15.7 us
    all_to_all x1, starting transfers between devices, per_device(): lax.all_to_all(expo_float.astype(jnp.bfloat16), 'outer', split_axis=0, co...  10.1 us
    unnamed x5, local copies, waits for them, and re-layouts  4.48 us
  transfers between devices with their start and end apart: 3, of which 3 were waited for; matrix products, arithmetic and copies ran while one was open for 2% of the time, Pallas kernels for 0%

commit v1 on v0

v1 whole, which is shorter than its diff:
```python
import jax
import jax.numpy as jnp
import numpy as np
from jax import lax
from jax.experimental import pallas as pl
from jax.experimental.pallas import tpu as pltpu
from jax.sharding import Mesh
from jax.sharding import PartitionSpec as P

SIZES = (("zl", 4), ("c", 2), ("x", 4), ("zh", 2), ("y", 8))


def hadamard(width):
    index = np.arange(width)
    common = index[:, None] & index[None, :]
    parity = np.zeros((width, width), np.int32)
    for bit in range(width.bit_length() - 1):
        parity = parity + (common >> bit & 1)
    return (1 - 2 * (parity % 2)).astype(np.float32)


def exact_dot(values, table):
    total = None
    for _ in range(3):
        part = values.astype(jnp.bfloat16)
        values = values - part.astype(jnp.float32)
        product = jnp.dot(part, table, preferred_element_type=jnp.float32)
        total = product if total is None else total + product
    return total


def encode_kernel(grad_ref, expo_ref, bits_ref, table_ref, out_ref):
    width = grad_ref.shape[1]
    sign = (2 * bits_ref[...] - 1).astype(jnp.float32)
    rotated = exact_dot(grad_ref[...] * sign, table_ref[...]) * (width**-0.5)
    limit = 4.0 * jnp.exp2(expo_ref[...].astype(jnp.float32))
    out_ref[...] = jnp.clip(rotated, -limit, limit).astype(out_ref.dtype)


def update_kernel(terms_ref, bits_ref, params_ref, momentum_ref, expo_ref, table_ref,
                  new_params_ref, new_momentum_ref, codes_ref):
    replicas, _, width = terms_ref.shape
    total = terms_ref[0].astype(jnp.float32)
    for replica in range(1, replicas):
        total = total + terms_ref[replica].astype(jnp.float32)
    sign = (2 * bits_ref[...] - 1).astype(jnp.float32)
    delta = exact_dot(total, table_ref[...]) * sign * (width**-0.5 / replicas)
    new_momentum = 0.9 * momentum_ref[...] + delta
    new_params = params_ref[...] - 0.7 * (delta + 0.9 * new_momentum)
    new_momentum_ref[...] = new_momentum
    new_params_ref[...] = new_params
    inverse = jnp.exp2(-expo_ref[...].astype(jnp.float32))
    codes = jnp.clip(new_params * inverse, -4.0, 4.0).astype(codes_ref.dtype)
    codes_ref[...] = jnp.broadcast_to(codes[None], codes_ref.shape)


def shift(value, axis, by):
    size = lax.axis_size(axis)
    return lax.ppermute(value, axis, [(i, (i + by) % size) for i in range(size)])


def per_device(pseudo_grad, grad_expo, sign_bits, params, momentum, param_expo):
    shard, width = sign_bits.shape
    owned = params.shape[0]
    replicas = lax.axis_size(("zl", "c"))
    table = jnp.asarray(hadamard(width), jnp.bfloat16)
    vmem = pl.BlockSpec(memory_space=pltpu.VMEM)

    terms = pl.pallas_call(
        encode_kernel,
        out_shape=jax.ShapeDtypeStruct((shard, width), jnp.bfloat16),
        in_specs=[vmem] * 4,
        out_specs=vmem,
    )(pseudo_grad[0], grad_expo[0][:, None], sign_bits, table)
    terms = lax.all_to_all(terms, ("zl", "c"), split_axis=0, concat_axis=0, tiled=True)

    me = lax.axis_index(("zl", "c"))
    own_bits = lax.dynamic_slice_in_dim(sign_bits, me * owned, owned, 0)
    line = ("zh", "y", "zl")
    chips = lax.axis_size(line)
    new_params, new_momentum, spread = pl.pallas_call(
        update_kernel,
        out_shape=(
            jax.ShapeDtypeStruct((owned, width), jnp.float32),
            jax.ShapeDtypeStruct((owned, width), jnp.float32),
            jax.ShapeDtypeStruct((chips, owned, width), jnp.bfloat16),
        ),
        in_specs=[vmem] * 6,
        out_specs=(vmem,) * 3,
    )(terms.reshape(replicas, owned, width), own_bits, params, momentum, param_expo[:, None], table)

    plane = lax.all_to_all(spread, line, split_axis=0, concat_axis=0, tiled=True)
    planes = lax.axis_size("x")
    x, core = lax.axis_index("x"), lax.axis_index("c")
    whole = jnp.zeros((planes, chips, 2, owned, width), jnp.bfloat16)
    for by in (0, 1, -1, 2):
        mine = plane if by == 0 else shift(plane, "x", by)
        other = shift(mine, "c", 1)
        at = lax.rem(x - by + planes, planes)
        for side, piece in ((core, mine), (1 - core, other)):
            whole = lax.dynamic_update_slice(
                whole, piece[None, :, None], (at, 0, side, 0, 0)
            )
    return new_params, new_momentum, whole.reshape(-1, width)


def solution(mesh):
    names, sizes = zip(*SIZES)
    cut = Mesh(mesh.devices.reshape(sizes), names)
    outer, dev = ("zl", "c"), ("x", "zh", "y")
    owner = dev + outer
    in_specs = (P(outer, dev, None), P(outer, dev), P(dev, None),
                P(owner, None), P(owner, None), P(owner))
    out_specs = (P(owner, None), P(owner, None), P())
    return jax.shard_map(
        per_device, mesh=cut, in_specs=in_specs, out_specs=out_specs, check_vma=False
    )
```

time: 219 us -> 90.1 us (0.41)
  waiting for transfers between devices: 161 us -> 3.4 us
  starting transfers between devices: 14.2 us -> 43.3 us
  blocking collectives: 15.7 us -> 29.7 us
  between operations: 14.1 us -> 0.86 us
  Pallas kernels: 0 us -> 3.94 us
  other arithmetic: 3.59 us -> 0 us
  matrix products: 2.83 us -> 0 us
  local copies, waits for them, and re-layouts: 5.24 us -> 7.99 us
    all_gather x1 -> x0, waiting for transfers between devices: 155 us -> none  [per_device(): fragment_codes = lax.all_gather(shard_codes, 'dev', axis=0, tiled=True)]
    ppermute x0 -> x7, starting transfers between devices: none -> 33.2 us  [shift(): lax.ppermute(value, axis, [(i, (i + by) % size) for i in range(size)])]
    all_to_all x0 -> x1, blocking collectives: none -> 29.7 us  [per_device(): lax.all_to_all(spread, line, split_axis=0, concat_axis=0, tiled=True)]
    all_gather x1 -> x0, blocking collectives: 15.7 us -> none  [per_device(): shard_codes = lax.all_gather(own_codes, 'outer', axis=0, tiled=True)]
    all_to_all x2 -> x1, starting transfers between devices: 14.2 us -> 10.1 us  [per_device(): lax.all_to_all(terms, ('zl', 'c'), split_axis=0, concat_axis=0, tiled=True)]
    pallas_call x0 -> x2, Pallas kernels: none -> 3.94 us  [the longest x1 2.03 us: per_device(): pl.pallas_call(update_kernel, out_shape=(jax.ShapeDtypeStruct((owned, wid...]
    all_to_all x2 -> x1, waiting for transfers between devices: 5.31 us -> 2.46 us  [per_device(): lax.all_to_all(terms, ('zl', 'c'), split_axis=0, concat_axis=0, tiled=True)]
    dot_general x2 -> x0, matrix products: 2.83 us -> none  [the longest x1 2.23 us: per_device(): jnp.dot(pseudo_grad[0] * sign, table, precision=lax.Precision.HIGHEST)]
  transfers between devices with their start and end apart: 3 -> 8, of which waited for: 3 -> 2; matrix products, arithmetic and copies ran while one was open for 2% -> 4% of each run, Pallas kernels for 0% -> 0%
where the time goes in v1:
time: 90.1 us; the launch traced here: 89.2 us
  starting transfers between devices  43.3 us (48%)
  blocking collectives  29.7 us (33%)
  local copies, waits for them, and re-layouts  7.99 us (9%)
  Pallas kernels  3.94 us (4%)
  waiting for transfers between devices  3.4 us (4%)
    ppermute x7, starting transfers between devices, shift(): lax.ppermute(value, axis, [(i, (i + by) % size) for i in range(size)])  33.2 us
    all_to_all x1, blocking collectives, per_device(): lax.all_to_all(spread, line, split_axis=0, concat_axis=0, tiled=True)  29.7 us
    all_to_all x1, starting transfers between devices, per_device(): lax.all_to_all(terms, ('zl', 'c'), split_axis=0, concat_axis=0, tiled=True)  10.1 us
    unnamed x4, local copies, waits for them, and re-layouts  2.63 us
    all_to_all x1, waiting for transfers between devices, per_device(): lax.all_to_all(terms, ('zl', 'c'), split_axis=0, concat_axis=0, tiled=True)  2.46 us
    pallas_call x1, Pallas kernels, per_device(): pl.pallas_call(update_kernel, out_shape=(jax.ShapeDtypeStruct((owned, wid...  2.03 us
    pallas_call x1, Pallas kernels, per_device(): pl.pallas_call(encode_kernel, out_shape=jax.ShapeDtypeStruct((shard, widt...  1.92 us
  transfers between devices with their start and end apart: 8, of which 2 were waited for; matrix products, arithmetic and copies ran while one was open for 4% of the time, Pallas kernels for 0%

profile of v1, /device:TPU:1, one launch (start us, length us, event | category | flops | bytes accessed | tf_op | source)
XLA Modules:
  0.0 89.2 jit_solution(9854715835698924990)
XLA Ops:
  0.6 1.4 %copy.10.expo_ref = s32[128,1]{1,0:T(8,128)} copy(s32[128,1]{0,1:T(1,128)} %bitcast.26) | data formatting | bytes 1024 | tf_op jit(solution)/shard_map/broadcast_in_dim;squeeze | solution.py:74
  2.0 1.9 %shard_map.94 = bf16[128,256]{1,0:T(8,128)(2,1)} custom-call(f32[128,256]{1,0:T(8,128)} %bitcast.25, s32[128,1]{1,0:T(8,128)} %copy.10.expo_ref, s32[128,256]{1,0:T(8,128)} %bits_ref.1, bf16[256,256]{1,0:T(8,128)(2,1)} %constant.50.clone.table_ref), custom_call_target="tpu_custom_call" | custom-call | tf_op jit(solution)/shard_map/pallas_call | solution.py:69
  3.9 10.1 %all-to-all-start = ((bf16[8,16,256]{2,1,0:T(8,128)(2,1)}), bf16[8,16,256]{2,1,0:T(8,128)(2,1)S(1)}, u32[]{:S(2)}, u32[]{:S(2)}) async-start(bf16[8,16,256]{2,1,0:T(8,128)(2,1)} %bitcast.24), calls=%async_computation | async-start | bytes 131072 | tf_op jit(solution)/shard_map/all_to_all | solution.py:75
  14.1 1.3 %copy.11.expo_ref = s32[16,1]{1,0:T(8,128)} copy(s32[16,1]{0,1:T(1,128)} %bitcast.27) | data formatting | bytes 128 | tf_op jit(solution)/shard_map/broadcast_in_dim | solution.py:90
  15.4 1.3 %constant_dynamic-slice_fusion.bits_ref = s32[16,256]{1,0:T(8,128)} fusion(s32[128,256]{1,0:T(8,128)} %bits_ref.1, s32[]{:T(128)S(6)} %select_n.14), kind=kLoop, calls=%fused_computation.8 | loop fusion | bytes 32772 | tf_op jit(solution)/shard_map/dynamic_slice | solution.py:78
  16.7 2.5 %all-to-all-done.terms_ref = bf16[8,16,256]{2,1,0:T(8,128)(2,1)S(1)} async-done(((bf16[8,16,256]{2,1,0:T(8,128)(2,1)}), bf16[8,16,256]{2,1,0:T(8,128)(2,1)S(1)}, u32[]{:S(2)}, u32[]{:S(2)}) %all-to-all-start) | async-done | bytes 65568 | tf_op jit(solution)/shard_map/all_to_all | solution.py:75
  19.2 0.6 copy-done.1
  19.8 2.0 %shard_map.95 = (f32[16,256]{1,0:T(8,128)}, f32[16,256]{1,0:T(8,128)}, bf16[64,16,256]{2,1,0:T(8,128)(2,1)}) custom-call(bf16[8,16,256]{2,1,0:T(8,128)(2,1)} %copy-done.1, s32[16,256]{1,0:T(8,128)} %constant_dynamic-slice_fusion.bits_ref, f32[16,256]{1,0:T(8,128)} %params_ref.1, f32[16,256]{1,0:T(8,128)} %momentum_ref.1, s32[16,1]{1,0:T(8,128)} %copy.11.expo_ref, ...), custom_call_target="tpu_custom_call" | custom-call | tf_op jit(solution)/shard_map/pallas_call | solution.py:81
  21.8 29.7 %all_to_all.14 = bf16[64,16,256]{2,1,0:T(8,128)(2,1)S(1)} all-to-all(bf16[64,16,256]{2,1,0:T(8,128)(2,1)} %get-tuple-element.8), channel_id=1, replica_groups=mesh['zl'=4,'c'=2,'x'=4,'zh'=2,'y'=8] {'zh','y','zl'}, dimensions={0} | all-to-all | bytes 1048576 | tf_op jit(solution)/shard_map/all_to_all | solution.py:92
  51.5 3.1 %collective-permute-start.1 = (bf16[64,16,256]{2,1,0:T(8,128)(2,1)S(1)}, bf16[64,16,256]{2,1,0:T(8,128)(2,1)S(1)}, u32[]{:S(2)}, u32[]{:S(2)}) collective-permute-start(bf16[64,16,256]{2,1,0:T(8,128)(2,1)S(1)} %all_to_all.14), channel_id=1, source_target_pairs={{0,16},{16,32},{32,48},{48,0},{1,17},{17,33},{33,49},{49,1},{2,18}... | collective-permute-start | bytes 1572872 | tf_op jit(solution)/shard_map/ppermute | solution.py:59
  54.6 3.4 %collective-permute-start.3 = (bf16[64,16,256]{2,1,0:T(8,128)(2,1)S(1)}, bf16[64,16,256]{2,1,0:T(8,128)(2,1)S(1)}, u32[]{:S(2)}, u32[]{:S(2)}) collective-permute-start(bf16[64,16,256]{2,1,0:T(8,128)(2,1)S(1)} %all_to_all.14), channel_id=1, source_target_pairs={{0,48},{16,0},{32,16},{48,32},{1,49},{17,1},{33,17},{49,33},{2,50}... | collective-permute-start | bytes 1572872 | tf_op jit(solution)/shard_map/ppermute | solution.py:59
  58.0 3.4 %collective-permute-start.5 = (bf16[64,16,256]{2,1,0:T(8,128)(2,1)S(1)}, bf16[64,16,256]{2,1,0:T(8,128)(2,1)S(1)}, u32[]{:S(2)}, u32[]{:S(2)}) collective-permute-start(bf16[64,16,256]{2,1,0:T(8,128)(2,1)S(1)} %all_to_all.14), channel_id=1, source_target_pairs={{0,32},{16,48},{32,0},{48,16},{1,33},{17,49},{33,1},{49,17},{2,34}... | collective-permute-start | bytes 1572872 | tf_op jit(solution)/shard_map/ppermute | solution.py:59
  61.4 6.1 %collective-permute-start = (bf16[64,16,256]{2,1,0:T(8,128)(2,1)S(1)}, bf16[64,16,256]{2,1,0:T(8,128)(2,1)S(1)}, u32[]{:S(2)}, u32[]{:S(2)}) collective-permute-start(bf16[64,16,256]{2,1,0:T(8,128)(2,1)S(1)} %all_to_all.14), channel_id=1, source_target_pairs={{0,64},{64,0},{1,65},{65,1},{2,66},{66,2},{3,67},{67,3},{4,68},{68... | collective-permute-start | bytes 1572872 | tf_op jit(solution)/shard_map/ppermute | solution.py:59
  67.5 6.1 %collective-permute-start.2 = (bf16[64,16,256]{2,1,0:T(8,128)(2,1)S(1)}, bf16[64,16,256]{2,1,0:T(8,128)(2,1)S(1)}, u32[]{:S(2)}, u32[]{:S(2)}) collective-permute-start(bf16[64,16,256]{2,1,0:T(8,128)(2,1)S(1)} %collective-permute-done.1), channel_id=1, source_target_pairs={{0,64},{64,0},{1,65},{65,1},{2,66},{66,2},{3,67},{67,3},{4,68},{68... | collective-permute-start | bytes 1572872 | tf_op jit(solution)/shard_map/ppermute | solution.py:59
  73.7 0.4 broadcast_in_dim.31
  74.1 0.0 collective-permute-done.3
  74.1 9.2 %collective-permute-start.4 = (bf16[64,16,256]{2,1,0:T(8,128)(2,1)S(1)}, bf16[64,16,256]{2,1,0:T(8,128)(2,1)S(1)}, u32[]{:S(2)}, u32[]{:S(2)}) collective-permute-start(bf16[64,16,256]{2,1,0:T(8,128)(2,1)S(1)} %collective-permute-done.3), channel_id=1, source_target_pairs={{0,64},{64,0},{1,65},{65,1},{2,66},{66,2},{3,67},{67,3},{4,68},{68... | collective-permute-start | bytes 1572872 | tf_op jit(solution)/shard_map/ppermute | solution.py:59
  83.3 0.0 collective-permute-done.5
  83.3 1.9 %collective-permute-start.6 = (bf16[64,16,256]{2,1,0:T(8,128)(2,1)S(1)}, bf16[64,16,256]{2,1,0:T(8,128)(2,1)S(1)}, u32[]{:S(2)}, u32[]{:S(2)}) collective-permute-start(bf16[64,16,256]{2,1,0:T(8,128)(2,1)S(1)} %collective-permute-done.5), channel_id=1, source_target_pairs={{0,64},{64,0},{1,65},{65,1},{2,66},{66,2},{3,67},{67,3},{4,68},{68... | collective-permute-start | bytes 1572872 | tf_op jit(solution)/shard_map/ppermute | solution.py:59
  85.5 0.6 copy.12
  86.1 0.9 %collective-permute-done.6 = bf16[64,16,256]{2,1,0:T(8,128)(2,1)S(1)} collective-permute-done((bf16[64,16,256]{2,1,0:T(8,128)(2,1)S(1)}, bf16[64,16,256]{2,1,0:T(8,128)(2,1)S(1)}, u32[]{:S(2)}, u32[]{:S(2)}) %collective-permute-start.6) | collective-permute-done | bytes 524320 | tf_op jit(solution)/shard_map/ppermute | solution.py:59
  87.1 0.1 bitcast_dynamic-update-slice_fusion
  87.1 0.0 copy-start
  87.2 2.0 %copy-done = bf16[4,64,2,16,256]{4,3,2,1,0:T(8,128)(2,1)} copy-done((bf16[4,64,2,16,256]{4,3,2,1,0:T(8,128)(2,1)}, bf16[4,64,2,16,256]{4,3,2,1,0:T(8,128)(2,1)S(1)}, u32[]{:S(2)}) %copy-start) | copy-done | bytes 4194328
  (12 shorter events, 0.3 us)
Async XLA Ops:
  3.9 15.2 %all-to-all-start = ((bf16[8,16,256]{2,1,0:T(8,128)(2,1)}), bf16[8,16,256]{2,1,0:T(8,128)(2,1)S(1)}, u32[]{:S(2)}, u32[]{:S(2)}) async-start(bf16[8,16,256]{2,1,0:T(8,128)(2,1)} %bitcast.24), calls=%async_computation | async-start | bytes 131072 | tf_op jit(solution)/shard_map/all_to_all | solution.py:75
  19.2 0.6 copy-start.1
  51.5 16.0 %collective-permute-start.1 = (bf16[64,16,256]{2,1,0:T(8,128)(2,1)S(1)}, bf16[64,16,256]{2,1,0:T(8,128)(2,1)S(1)}, u32[]{:S(2)}, u32[]{:S(2)}) collective-permute-start(bf16[64,16,256]{2,1,0:T(8,128)(2,1)S(1)} %all_to_all.14), channel_id=1, source_target_pairs={{0,16},{16,32},{32,48},{48,0},{1,17},{17,33},{33,49},{49,1},{2,18}... | collective-permute-start | bytes 1572872 | tf_op jit(solution)/shard_map/ppermute | solution.py:59
  54.6 19.5 %collective-permute-start.3 = (bf16[64,16,256]{2,1,0:T(8,128)(2,1)S(1)}, bf16[64,16,256]{2,1,0:T(8,128)(2,1)S(1)}, u32[]{:S(2)}, u32[]{:S(2)}) collective-permute-start(bf16[64,16,256]{2,1,0:T(8,128)(2,1)S(1)} %all_to_all.14), channel_id=1, source_target_pairs={{0,48},{16,0},{32,16},{48,32},{1,49},{17,1},{33,17},{49,33},{2,50}... | collective-permute-start | bytes 1572872 | tf_op jit(solution)/shard_map/ppermute | solution.py:59
  58.0 25.3 %collective-permute-start.5 = (bf16[64,16,256]{2,1,0:T(8,128)(2,1)S(1)}, bf16[64,16,256]{2,1,0:T(8,128)(2,1)S(1)}, u32[]{:S(2)}, u32[]{:S(2)}) collective-permute-start(bf16[64,16,256]{2,1,0:T(8,128)(2,1)S(1)} %all_to_all.14), channel_id=1, source_target_pairs={{0,32},{16,48},{32,0},{48,16},{1,33},{17,49},{33,1},{49,17},{2,34}... | collective-permute-start | bytes 1572872 | tf_op jit(solution)/shard_map/ppermute | solution.py:59
  61.4 23.8 %collective-permute-start = (bf16[64,16,256]{2,1,0:T(8,128)(2,1)S(1)}, bf16[64,16,256]{2,1,0:T(8,128)(2,1)S(1)}, u32[]{:S(2)}, u32[]{:S(2)}) collective-permute-start(bf16[64,16,256]{2,1,0:T(8,128)(2,1)S(1)} %all_to_all.14), channel_id=1, source_target_pairs={{0,64},{64,0},{1,65},{65,1},{2,66},{66,2},{3,67},{67,3},{4,68},{68... | collective-permute-start | bytes 1572872 | tf_op jit(solution)/shard_map/ppermute | solution.py:59
  67.5 17.8 %collective-permute-start.2 = (bf16[64,16,256]{2,1,0:T(8,128)(2,1)S(1)}, bf16[64,16,256]{2,1,0:T(8,128)(2,1)S(1)}, u32[]{:S(2)}, u32[]{:S(2)}) collective-permute-start(bf16[64,16,256]{2,1,0:T(8,128)(2,1)S(1)} %collective-permute-done.1), channel_id=1, source_target_pairs={{0,64},{64,0},{1,65},{65,1},{2,66},{66,2},{3,67},{67,3},{4,68},{68... | collective-permute-start | bytes 1572872 | tf_op jit(solution)/shard_map/ppermute | solution.py:59
  74.1 11.3 %collective-permute-start.4 = (bf16[64,16,256]{2,1,0:T(8,128)(2,1)S(1)}, bf16[64,16,256]{2,1,0:T(8,128)(2,1)S(1)}, u32[]{:S(2)}, u32[]{:S(2)}) collective-permute-start(bf16[64,16,256]{2,1,0:T(8,128)(2,1)S(1)} %collective-permute-done.3), channel_id=1, source_target_pairs={{0,64},{64,0},{1,65},{65,1},{2,66},{66,2},{3,67},{67,3},{4,68},{68... | collective-permute-start | bytes 1572872 | tf_op jit(solution)/shard_map/ppermute | solution.py:59
  83.3 3.8 %collective-permute-start.6 = (bf16[64,16,256]{2,1,0:T(8,128)(2,1)S(1)}, bf16[64,16,256]{2,1,0:T(8,128)(2,1)S(1)}, u32[]{:S(2)}, u32[]{:S(2)}) collective-permute-start(bf16[64,16,256]{2,1,0:T(8,128)(2,1)S(1)} %collective-permute-done.5), channel_id=1, source_target_pairs={{0,64},{64,0},{1,65},{65,1},{2,66},{66,2},{3,67},{67,3},{4,68},{68... | collective-permute-start | bytes 1572872 | tf_op jit(solution)/shard_map/ppermute | solution.py:59
  87.1 2.0 %copy-start = (bf16[4,64,2,16,256]{4,3,2,1,0:T(8,128)(2,1)}, bf16[4,64,2,16,256]{4,3,2,1,0:T(8,128)(2,1)S(1)}, u32[]{:S(2)}) copy-start(bf16[4,64,2,16,256]{4,3,2,1,0:T(8,128)(2,1)S(1)} %bitcast_dynamic-update-slice_fusion) | copy-start | bytes 12582916

commit v2 on v1

--- a/solution.py
+++ b/solution.py
@@ -8,6 +8,44 @@
 from jax.sharding import PartitionSpec as P
 
 SIZES = (("zl", 4), ("c", 2), ("x", 4), ("zh", 2), ("y", 8))
+AXES = tuple(name for name, _ in SIZES)
+BITS = (0, 1)
+
+
+def device(x, y, z, core):
+    x, y, z = x % 4, y % 8, z % 8
+    return (((z % 4 * 2 + core) * 4 + x) * 2 + z // 4) * 8 + y
+
+
+def classes():
+    return [
+        [
+            device(2 * xh + px, 2 * yh + py, 4 * zh + 2 * zm + pz, core)
+            for xh in BITS
+            for zh in BITS
+            for yh in range(4)
+            for zm in BITS
+        ]
+        for px in BITS
+        for py in BITS
+        for pz in BITS
+        for core in BITS
+    ]
+
+
+def cubes():
+    return [
+        [
+            device(2 * xh + way * px, 2 * yh + way * py, 2 * zm + way * pz, core)
+            for px in BITS
+            for py in BITS
+            for pz in BITS
+        ]
+        for core, way in ((0, 1), (1, -1))
+        for xh in range(2)
+        for yh in range(4)
+        for zm in range(4)
+    ]
 
 
 def hadamard(width):
@@ -50,13 +88,56 @@
     new_momentum_ref[...] = new_momentum
     new_params_ref[...] = new_params
     inverse = jnp.exp2(-expo_ref[...].astype(jnp.float32))
-    codes = jnp.clip(new_params * inverse, -4.0, 4.0).astype(codes_ref.dtype)
-    codes_ref[...] = jnp.broadcast_to(codes[None], codes_ref.shape)
+    codes_ref[...] = jnp.clip(new_params * inverse, -4.0, 4.0).astype(codes_ref.dtype)
 
 
-def shift(value, axis, by):
-    size = lax.axis_size(axis)
-    return lax.ppermute(value, axis, [(i, (i + by) % size) for i in range(size)])
+def place_kernel(side_ref, part_ref, *refs):
+    out_ref, sems = refs[-2:]
+    side = side_ref[0]
+    copies = []
+    for px in BITS:
+        for py in BITS:
+            for pz in BITS:
+                for xh in BITS:
+                    for zh in BITS:
+                        copies.append(
+                            pltpu.make_async_copy(
+                                part_ref.at[px, py, pz, xh, zh],
+                                out_ref.at[2 * xh + px, zh, :, py, :, pz, side],
+                                sems.at[len(copies)],
+                            )
+                        )
+    for copy in copies:
+        copy.start()
+    for copy in copies:
+        copy.wait()
+
+
+def place(side, part, whole=None):
+    owned, width = part.shape[-2:]
+    shape = jax.ShapeDtypeStruct((4, 2, 4, 2, 2, 2, 2, owned, width), part.dtype)
+    given = (side, part) if whole is None else (side, part, whole)
+    smem = pl.BlockSpec(memory_space=pltpu.SMEM)
+    anywhere = pl.BlockSpec(memory_space=pl.ANY)
+    return pl.pallas_call(
+        place_kernel,
+        out_shape=shape,
+        in_specs=[smem] + [anywhere] * (len(given) - 1),
+        out_specs=anywhere,
+        scratch_shapes=[pltpu.SemaphoreType.DMA((32,))],
+        input_output_aliases={} if whole is None else {2: 0},
+        cost_estimate=pl.CostEstimate(
+            flops=0, bytes_accessed=2 * part.size * 2, transcendentals=0
+        ),
+    )(*given)
+
+
+def gather(value, groups):
+    copies = jnp.broadcast_to(value[None], (len(groups[0]),) + value.shape)
+    return lax.all_to_all(
+        copies.reshape((-1,) + value.shape[1:]), AXES, split_axis=0, concat_axis=0,
+        axis_index_groups=groups, tiled=True,
+    )
 
 
 def per_device(pseudo_grad, grad_expo, sign_bits, params, momentum, param_expo):
@@ -76,31 +157,23 @@
 
     me = lax.axis_index(("zl", "c"))
     own_bits = lax.dynamic_slice_in_dim(sign_bits, me * owned, owned, 0)
-    line = ("zh", "y", "zl")
-    chips = lax.axis_size(line)
-    new_params, new_momentum, spread = pl.pallas_call(
+    new_params, new_momentum, codes = pl.pallas_call(
         update_kernel,
         out_shape=(
             jax.ShapeDtypeStruct((owned, width), jnp.float32),
             jax.ShapeDtypeStruct((owned, width), jnp.float32),
-            jax.ShapeDtypeStruct((chips, owned, width), jnp.bfloat16),
+            jax.ShapeDtypeStruct((owned, width), jnp.bfloat16),
         ),
         in_specs=[vmem] * 6,
         out_specs=(vmem,) * 3,
     )(terms.reshape(replicas, owned, width), own_bits, params, momentum, param_expo[:, None], table)
 
-    plane = lax.all_to_all(spread, line, split_axis=0, concat_axis=0, tiled=True)
-    planes = lax.axis_size("x")
-    x, core = lax.axis_index("x"), lax.axis_index("c")
-    whole = jnp.zeros((planes, chips, 2, owned, width), jnp.bfloat16)
-    for by in (0, 1, -1, 2):
-        mine = plane if by == 0 else shift(plane, "x", by)
-        other = shift(mine, "c", 1)
-        at = lax.rem(x - by + planes, planes)
-        for side, piece in ((core, mine), (1 - core, other)):
-            whole = lax.dynamic_update_slice(
-                whole, piece[None, :, None], (at, 0, side, 0, 0)
-            )
+    mine = gather(gather(codes, classes()), cubes())
+    other = lax.ppermute(mine, "c", [(0, 1), (1, 0)])
+    parts = (2, 2, 2, 2, 2, 4, 2, owned, width)
+    core = lax.axis_index("c").astype(jnp.int32)[None]
+    whole = place(core, mine.reshape(parts))
+    whole = place(1 - core, other.reshape(parts), whole)
     return new_params, new_momentum, whole.reshape(-1, width)
 
 

time: 90.1 us -> 205 us (2.28)
  Pallas kernels: 3.94 us -> 134 us
  starting transfers between devices: 43.3 us -> 12 us
  blocking collectives: 29.7 us -> 50.6 us
  local copies, waits for them, and re-layouts: 7.99 us -> 5.51 us
    pallas_call x0 -> x2, Pallas kernels: none -> 130 us  [place(): pl.pallas_call(place_kernel, out_shape=shape, in_specs=[smem] + [anywhere...]
    ppermute x7 -> x1, starting transfers between devices: 33.2 us -> 1.91 us  [per_device(): other = lax.ppermute(mine, 'c', [(0, 1), (1, 0)])]
    all_to_all x1 -> x2, blocking collectives: 29.7 us -> 50.6 us  [gather(): lax.all_to_all(copies.reshape((-1,) + value.shape[1:]), AXES, split_axis=...]
  transfers between devices with their start and end apart: 8 -> 2, of which waited for: 2 -> 1; matrix products, arithmetic and copies ran while one was open for 4% -> 1% of each run, Pallas kernels for 0% -> 32%
where the time goes in v2:
time: 205 us
  Pallas kernels  134 us (65%)
  blocking collectives  50.6 us (25%)
  starting transfers between devices  12 us (6%)
  local copies, waits for them, and re-layouts  5.51 us (3%)
  waiting for transfers between devices  2.47 us (1%)
    pallas_call x2, Pallas kernels, place(): pl.pallas_call(place_kernel, out_shape=shape, in_specs=[smem] + [anywhere...  130 us
    all_to_all x2, blocking collectives, gather(): lax.all_to_all(copies.reshape((-1,) + value.shape[1:]), AXES, split_axis=...  50.6 us
    all_to_all x1, starting transfers between devices, per_device(): lax.all_to_all(terms, ('zl', 'c'), split_axis=0, concat_axis=0, tiled=True)  10.1 us
  transfers between devices with their start and end apart: 2, of which 1 were waited for; matrix products, arithmetic and copies ran while one was open for 1% of the time, Pallas kernels for 32%

profile of v2, /device:TPU:1, one launch (start us, length us, event | category | flops | bytes accessed | tf_op | source)
XLA Modules:
  0.0 204.9 jit_solution(16530305047707485657)
XLA Ops:
  0.6 1.4 copy.11.expo_ref
  2.0 1.9 shard_map.94
  3.9 10.1 %all-to-all-start = ((bf16[8,16,256]{2,1,0:T(8,128)(2,1)}), bf16[8,16,256]{2,1,0:T(8,128)(2,1)S(1)}, u32[]{:S(2)}, u32[]{:S(2)}) async-start(bf16[8,16,256]{2,1,0:T(8,128)(2,1)} %bitcast.14), calls=%async_computation | async-start | bytes 131072 | tf_op jit(solution)/shard_map/all_to_all | solution.py:156
  14.1 1.3 copy.12.expo_ref
  15.4 1.3 constant_dynamic-slice_fusion.bits_ref
  16.7 2.5 %all-to-all-done.terms_ref = bf16[8,16,256]{2,1,0:T(8,128)(2,1)S(1)} async-done(((bf16[8,16,256]{2,1,0:T(8,128)(2,1)}), bf16[8,16,256]{2,1,0:T(8,128)(2,1)S(1)}, u32[]{:S(2)}, u32[]{:S(2)}) %all-to-all-start) | async-done | bytes 65568 | tf_op jit(solution)/shard_map/all_to_all | solution.py:156
  19.2 0.0 copy-start.1
  19.2 0.6 copy-done.1
  19.8 1.8 shard_map.95
  21.6 0.7 broadcast_in_dim.22
  22.3 28.9 %all_to_all.24 = bf16[32,16,256]{2,1,0:T(8,128)(2,1)S(1)} all-to-all(bf16[32,16,256]{2,1,0:T(8,128)(2,1)S(1)} %broadcast_in_dim.22), channel_id=1, replica_groups={{0,256,2,258,4,260,6,262,8,264,10,266,12,268,14,270,32,288,34,290,36,29..., dimensions={0} | all-to-all | bytes 524288 | tf_op jit(solution)/shard_map/all_to_all | solution.py:137
  51.2 0.1 broadcast_in_dim.24
  51.3 21.7 %all_to_all.25 = bf16[8,512,256]{2,1,0:T(8,128)(2,1)S(1)} all-to-all(bf16[8,512,256]{2,1,0:T(8,128)(2,1)S(1)} %broadcast_in_dim.24), channel_id=1, replica_groups={{0,128,1,129,16,144,17,145},{256,384,257,385,272,400,273,401},{8,136,9,..., dimensions={0} | all-to-all | bytes 4194304 | tf_op jit(solution)/shard_map/all_to_all | solution.py:137
  73.1 0.0 copy-start
  73.1 1.9 collective-permute-start
  75.0 0.0 copy-done
  75.0 64.9 %shard_map.96.refs_0_ = bf16[4,2,4,2,2,2,2,16,256]{8,7,6,5,4,3,2,1,0:T(8,128)(2,1)} custom-call(s32[1]{0:T(128)} %bitcast.4.side_ref, bf16[2,2,2,2,2,4,2,16,256]{8,7,6,5,4,3,2,1,0:T(8,128)(2,1)} %bitcast.12), custom_call_target="tpu_custom_call" | custom-call | bytes 4194304 | tf_op jit(solution)/shard_map/pallas_call | solution.py:122
  139.9 0.0 collective-permute-done
  139.9 64.9 %shard_map.97 = bf16[4,2,4,2,2,2,2,16,256]{8,7,6,5,4,3,2,1,0:T(8,128)(2,1)} custom-call(s32[1]{0:T(128)S(6)} %sub.3.side_ref, bf16[2,2,2,2,2,4,2,16,256]{8,7,6,5,4,3,2,1,0:T(8,128)(2,1)} %bitcast.7.part_ref, bf16[4,2,4,2,2,2,2,16,256]{8,7,6,5,4,3,2,1,0:T(8,128)(2,1)} %shard_map.96.refs_0_), custom_call_target="tpu_custom_call", output_to_operand_aliasing={{}: (2, {})} | custom-call | bytes 4194304 | tf_op jit(solution)/shard_map/pallas_call | solution.py:122
Async XLA Ops:
  3.9 15.2 %all-to-all-start = ((bf16[8,16,256]{2,1,0:T(8,128)(2,1)}), bf16[8,16,256]{2,1,0:T(8,128)(2,1)S(1)}, u32[]{:S(2)}, u32[]{:S(2)}) async-start(bf16[8,16,256]{2,1,0:T(8,128)(2,1)} %bitcast.14), calls=%async_computation | async-start | bytes 131072 | tf_op jit(solution)/shard_map/all_to_all | solution.py:156
  19.2 0.6 copy-start.1
  73.1 1.9 copy-start
  73.1 66.9 %collective-permute-start = (bf16[4096,256]{1,0:T(8,128)(2,1)S(1)}, bf16[4096,256]{1,0:T(8,128)(2,1)}, u32[]{:S(2)}, u32[]{:S(2)}) collective-permute-start(bf16[4096,256]{1,0:T(8,128)(2,1)S(1)} %bitcast.11), channel_id=1, source_target_pairs={{0,64},{64,0},{1,65},{65,1},{2,66},{66,2},{3,67},{67,3},{4,68},{68... | collective-permute-start | bytes 6291464 | tf_op jit(solution)/shard_map/ppermute | solution.py:172

commit v3 on v2

--- a/solution.py
+++ b/solution.py
@@ -91,45 +91,30 @@
     codes_ref[...] = jnp.clip(new_params * inverse, -4.0, 4.0).astype(codes_ref.dtype)
 
 
-def place_kernel(side_ref, part_ref, *refs):
-    out_ref, sems = refs[-2:]
-    side = side_ref[0]
-    copies = []
-    for px in BITS:
+def place_kernel(core_ref, mine_ref, other_ref, out_ref):
+    x = pl.program_id(0)
+    core = core_ref[0]
+    for side, part_ref in ((core, mine_ref), (1 - core, other_ref)):
         for py in BITS:
             for pz in BITS:
-                for xh in BITS:
-                    for zh in BITS:
-                        copies.append(
-                            pltpu.make_async_copy(
-                                part_ref.at[px, py, pz, xh, zh],
-                                out_ref.at[2 * xh + px, zh, :, py, :, pz, side],
-                                sems.at[len(copies)],
-                            )
-                        )
-    for copy in copies:
-        copy.start()
-    for copy in copies:
-        copy.wait()
+                out_ref[0, :, :, py, :, pz, side] = part_ref[x % 2, py, pz, x // 2]
 
 
-def place(side, part, whole=None):
-    owned, width = part.shape[-2:]
-    shape = jax.ShapeDtypeStruct((4, 2, 4, 2, 2, 2, 2, owned, width), part.dtype)
-    given = (side, part) if whole is None else (side, part, whole)
-    smem = pl.BlockSpec(memory_space=pltpu.SMEM)
-    anywhere = pl.BlockSpec(memory_space=pl.ANY)
+def place(core, mine, other):
+    owned, width = mine.shape[-2:]
+    block = (2, 4, 2, 2, 2, 2, owned, width)
+    vmem = pl.BlockSpec(memory_space=pltpu.VMEM)
     return pl.pallas_call(
         place_kernel,
-        out_shape=shape,
-        in_specs=[smem] + [anywhere] * (len(given) - 1),
-        out_specs=anywhere,
-        scratch_shapes=[pltpu.SemaphoreType.DMA((32,))],
-        input_output_aliases={} if whole is None else {2: 0},
+        out_shape=jax.ShapeDtypeStruct((4,) + block, mine.dtype),
+        grid=(4,),
+        in_specs=[pl.BlockSpec(memory_space=pltpu.SMEM), vmem, vmem],
+        out_specs=pl.BlockSpec((1,) + block, lambda x: (x,) + (0,) * len(block)),
         cost_estimate=pl.CostEstimate(
-            flops=0, bytes_accessed=2 * part.size * 2, transcendentals=0
+            flops=0, bytes_accessed=8 * mine.size, transcendentals=0
         ),
-    )(*given)
+        compiler_params=pltpu.CompilerParams(vmem_limit_bytes=16 * 2**20),
+    )(core, mine, other)
 
 
 def gather(value, groups):
@@ -172,8 +157,7 @@
     other = lax.ppermute(mine, "c", [(0, 1), (1, 0)])
     parts = (2, 2, 2, 2, 2, 4, 2, owned, width)
     core = lax.axis_index("c").astype(jnp.int32)[None]
-    whole = place(core, mine.reshape(parts))
-    whole = place(1 - core, other.reshape(parts), whole)
+    whole = place(core, mine.reshape(parts), other.reshape(parts))
     return new_params, new_momentum, whole.reshape(-1, width)
 
 

time: 205 us -> 82 us (0.40)
  Pallas kernels: 134 us -> 6.16 us
  waiting for transfers between devices: 2.47 us -> 6.59 us
    pallas_call x2 -> x1, Pallas kernels: 130 us -> 2.44 us  [place(): pl.pallas_call(place_kernel, out_shape=jax.ShapeDtypeStruct((4,) + block,...]
    ppermute x1, waiting for transfers between devices: 0.01 us -> 4.13 us  [per_device(): other = lax.ppermute(mine, 'c', [(0, 1), (1, 0)])]
  transfers between devices with their start and end apart: 2 -> 2, of which waited for: 1 -> 2; matrix products, arithmetic and copies ran while one was open for 1% -> 3% of each run, Pallas kernels for 32% -> 0%
where the time goes in v3:
time: 82 us; the launch traced here: 81.5 us
  blocking collectives  50.6 us (62%)
  starting transfers between devices  12 us (15%)
  waiting for transfers between devices  6.59 us (8%)
  Pallas kernels  6.16 us (8%)
  local copies, waits for them, and re-layouts  5.51 us (7%)
    all_to_all x2, blocking collectives, gather(): lax.all_to_all(copies.reshape((-1,) + value.shape[1:]), AXES, split_axis=...  50.6 us
    all_to_all x1, starting transfers between devices, per_device(): lax.all_to_all(terms, ('zl', 'c'), split_axis=0, concat_axis=0, tiled=True)  10.1 us
    ppermute x1, waiting for transfers between devices, per_device(): other = lax.ppermute(mine, 'c', [(0, 1), (1, 0)])  4.13 us
    all_to_all x1, waiting for transfers between devices, per_device(): lax.all_to_all(terms, ('zl', 'c'), split_axis=0, concat_axis=0, tiled=True)  2.47 us
    pallas_call x1, Pallas kernels, place(): pl.pallas_call(place_kernel, out_shape=jax.ShapeDtypeStruct((4,) + block,...  2.44 us
    pallas_call x1, Pallas kernels, per_device(): pl.pallas_call(encode_kernel, out_shape=jax.ShapeDtypeStruct((shard, widt...  1.92 us
    ppermute x1, starting transfers between devices, per_device(): other = lax.ppermute(mine, 'c', [(0, 1), (1, 0)])  1.91 us
    pallas_call x1, Pallas kernels, per_device(): pl.pallas_call(update_kernel, out_shape=(jax.ShapeDtypeStruct((owned, wid...  1.8 us
  transfers between devices with their start and end apart: 2, of which 2 were waited for; matrix products, arithmetic and copies ran while one was open for 3% of the time, Pallas kernels for 0%

profile of v3, /device:TPU:1, one launch (start us, length us, event | category | flops | bytes accessed | tf_op | source)
XLA Modules:
  0.0 81.5 jit_solution(2065805666377152631)
XLA Ops:
  0.6 1.4 %copy.10.expo_ref = s32[128,1]{1,0:T(8,128)} copy(s32[128,1]{0,1:T(1,128)} %bitcast.17) | data formatting | bytes 1024 | tf_op jit(solution)/shard_map/broadcast_in_dim;squeeze | solution.py:140
  2.0 1.9 %shard_map.94 = bf16[128,256]{1,0:T(8,128)(2,1)} custom-call(f32[128,256]{1,0:T(8,128)} %bitcast.16, s32[128,1]{1,0:T(8,128)} %copy.10.expo_ref, s32[128,256]{1,0:T(8,128)} %bits_ref.1, bf16[256,256]{1,0:T(8,128)(2,1)} %constant.22.clone.table_ref), custom_call_target="tpu_custom_call" | custom-call | tf_op jit(solution)/shard_map/pallas_call | solution.py:135
  3.9 10.1 %all-to-all-start = ((bf16[8,16,256]{2,1,0:T(8,128)(2,1)}), bf16[8,16,256]{2,1,0:T(8,128)(2,1)S(1)}, u32[]{:S(2)}, u32[]{:S(2)}) async-start(bf16[8,16,256]{2,1,0:T(8,128)(2,1)} %bitcast.15), calls=%async_computation | async-start | bytes 131072 | tf_op jit(solution)/shard_map/all_to_all | solution.py:141
  14.1 1.3 %copy.11.expo_ref = s32[16,1]{1,0:T(8,128)} copy(s32[16,1]{0,1:T(1,128)} %bitcast.18) | data formatting | bytes 128 | tf_op jit(solution)/shard_map/broadcast_in_dim | solution.py:154
  15.4 1.3 %constant_dynamic-slice_fusion.bits_ref = s32[16,256]{1,0:T(8,128)} fusion(s32[128,256]{1,0:T(8,128)} %bits_ref.1, s32[]{:T(128)S(6)} %select_n.3), kind=kLoop, calls=%fused_computation | loop fusion | bytes 32772 | tf_op jit(solution)/shard_map/dynamic_slice | solution.py:144
  16.7 2.5 %all-to-all-done.terms_ref = bf16[8,16,256]{2,1,0:T(8,128)(2,1)S(1)} async-done(((bf16[8,16,256]{2,1,0:T(8,128)(2,1)}), bf16[8,16,256]{2,1,0:T(8,128)(2,1)S(1)}, u32[]{:S(2)}, u32[]{:S(2)}) %all-to-all-start) | async-done | bytes 65568 | tf_op jit(solution)/shard_map/all_to_all | solution.py:141
  19.2 0.0 copy-start
  19.2 0.6 copy-done
  19.8 1.8 %shard_map.95 = (f32[16,256]{1,0:T(8,128)}, f32[16,256]{1,0:T(8,128)}, bf16[16,256]{1,0:T(8,128)(2,1)}) custom-call(bf16[8,16,256]{2,1,0:T(8,128)(2,1)} %copy-done, s32[16,256]{1,0:T(8,128)} %constant_dynamic-slice_fusion.bits_ref, f32[16,256]{1,0:T(8,128)} %params_ref.1, f32[16,256]{1,0:T(8,128)} %momentum_ref.1, s32[16,1]{1,0:T(8,128)} %copy.11.expo_ref, ...), custom_call_target="tpu_custom_call" | custom-call | tf_op jit(solution)/shard_map/pallas_call | solution.py:145
  21.6 0.7 broadcast_in_dim.22
  22.3 28.9 %all_to_all.24 = bf16[32,16,256]{2,1,0:T(8,128)(2,1)S(1)} all-to-all(bf16[32,16,256]{2,1,0:T(8,128)(2,1)S(1)} %broadcast_in_dim.22), channel_id=1, replica_groups={{0,256,2,258,4,260,6,262,8,264,10,266,12,268,14,270,32,288,34,290,36,29..., dimensions={0} | all-to-all | bytes 524288 | tf_op jit(solution)/shard_map/all_to_all | solution.py:122
  51.2 0.1 broadcast_in_dim.24
  51.3 21.7 %all_to_all.25 = bf16[8,512,256]{2,1,0:T(8,128)(2,1)S(1)} all-to-all(bf16[8,512,256]{2,1,0:T(8,128)(2,1)S(1)} %broadcast_in_dim.24), channel_id=1, replica_groups={{0,128,1,129,16,144,17,145},{256,384,257,385,272,400,273,401},{8,136,9,..., dimensions={0} | all-to-all | bytes 4194304 | tf_op jit(solution)/shard_map/all_to_all | solution.py:122
  73.1 1.9 %collective-permute-start = (bf16[4096,256]{1,0:T(8,128)(2,1)S(1)}, bf16[4096,256]{1,0:T(8,128)(2,1)S(1)}, u32[]{:S(2)}, u32[]{:S(2)}) collective-permute-start(bf16[4096,256]{1,0:T(8,128)(2,1)S(1)} %bitcast.10), channel_id=1, source_target_pairs={{0,64},{64,0},{1,65},{65,1},{2,66},{66,2},{3,67},{67,3},{4,68},{68... | collective-permute-start | bytes 6291464 | tf_op jit(solution)/shard_map/ppermute | solution.py:157
  75.0 4.1 %collective-permute-done = bf16[4096,256]{1,0:T(8,128)(2,1)S(1)} collective-permute-done((bf16[4096,256]{1,0:T(8,128)(2,1)S(1)}, bf16[4096,256]{1,0:T(8,128)(2,1)S(1)}, u32[]{:S(2)}, u32[]{:S(2)}) %collective-permute-start) | collective-permute-done | bytes 2097184 | tf_op jit(solution)/shard_map/ppermute | solution.py:157
  79.1 2.4 %shard_map.96 = bf16[4,2,4,2,2,2,2,16,256]{8,7,6,5,4,3,2,1,0:T(8,128)(2,1)} custom-call(s32[1]{0:T(128)} %bitcast.4.core_ref, bf16[2,2,2,2,2,4,2,16,256]{8,7,6,5,4,3,2,1,0:T(8,128)(2,1)S(1)} %bitcast.11, bf16[2,2,2,2,2,4,2,16,256]{8,7,6,5,4,3,2,1,0:T(8,128)(2,1)S(1)} %bitcast.12), custom_call_target="tpu_custom_call" | custom-call | bytes 8388608 | tf_op jit(solution)/shard_map/pallas_call | solution.py:107
Async XLA Ops:
  3.9 15.2 %all-to-all-start = ((bf16[8,16,256]{2,1,0:T(8,128)(2,1)}), bf16[8,16,256]{2,1,0:T(8,128)(2,1)S(1)}, u32[]{:S(2)}, u32[]{:S(2)}) async-start(bf16[8,16,256]{2,1,0:T(8,128)(2,1)} %bitcast.15), calls=%async_computation | async-start | bytes 131072 | tf_op jit(solution)/shard_map/all_to_all | solution.py:141
  19.2 0.6 copy-start
  73.1 6.0 %collective-permute-start = (bf16[4096,256]{1,0:T(8,128)(2,1)S(1)}, bf16[4096,256]{1,0:T(8,128)(2,1)S(1)}, u32[]{:S(2)}, u32[]{:S(2)}) collective-permute-start(bf16[4096,256]{1,0:T(8,128)(2,1)S(1)} %bitcast.10), channel_id=1, source_target_pairs={{0,64},{64,0},{1,65},{65,1},{2,66},{66,2},{3,67},{67,3},{4,68},{68... | collective-permute-start | bytes 6291464 | tf_op jit(solution)/shard_map/ppermute | solution.py:157

commit v4 on v3

--- a/solution.py
+++ b/solution.py
@@ -67,28 +67,80 @@
     return total
 
 
-def encode_kernel(grad_ref, expo_ref, bits_ref, table_ref, out_ref):
+def column(row):
+    n = row.shape[1]
+    down = lax.broadcasted_iota(jnp.int32, (n, n), 0)
+    along = lax.broadcasted_iota(jnp.int32, (n, n), 1)
+    spread = jnp.where(down == along, jnp.broadcast_to(row, (n, n)), 0.0)
+    return jnp.sum(spread, axis=1, keepdims=True)
+
+
+def encode_kernel(me_ref, grad_in, expo_in, bits_in, table_in, params_in, momentum_in,
+                  terms_ref, table_ref, params_ref, decayed_ref, own_sign_ref,
+                  grad_ref, expo_ref, bits_ref, momentum_ref, sems):
+    inward = (
+        (grad_in, grad_ref),
+        (expo_in, expo_ref),
+        (bits_in, bits_ref),
+        (table_in, table_ref),
+        (params_in, params_ref),
+        (momentum_in, momentum_ref),
+    )
+    copies = [
+        pltpu.make_async_copy(source, target, sems.at[i])
+        for i, (source, target) in enumerate(inward)
+    ]
+    for copy in copies:
+        copy.start()
+    for copy in copies:
+        copy.wait()
     width = grad_ref.shape[1]
+    owned = own_sign_ref.shape[0]
+    replicas = grad_ref.shape[0] // owned
     sign = (2 * bits_ref[...] - 1).astype(jnp.float32)
-    rotated = exact_dot(grad_ref[...] * sign, table_ref[...]) * (width**-0.5)
-    limit = 4.0 * jnp.exp2(expo_ref[...].astype(jnp.float32))
-    out_ref[...] = jnp.clip(rotated, -limit, limit).astype(out_ref.dtype)
-
-
-def update_kernel(terms_ref, bits_ref, params_ref, momentum_ref, expo_ref, table_ref,
-                  new_params_ref, new_momentum_ref, codes_ref):
-    replicas, _, width = terms_ref.shape
-    total = terms_ref[0].astype(jnp.float32)
-    for replica in range(1, replicas):
-        total = total + terms_ref[replica].astype(jnp.float32)
-    sign = (2 * bits_ref[...] - 1).astype(jnp.float32)
-    delta = exact_dot(total, table_ref[...]) * sign * (width**-0.5 / replicas)
-    new_momentum = 0.9 * momentum_ref[...] + delta
-    new_params = params_ref[...] - 0.7 * (delta + 0.9 * new_momentum)
-    new_momentum_ref[...] = new_momentum
-    new_params_ref[...] = new_params
-    inverse = jnp.exp2(-expo_ref[...].astype(jnp.float32))
-    codes_ref[...] = jnp.clip(new_params * inverse, -4.0, 4.0).astype(codes_ref.dtype)
+    table = table_ref[...].astype(jnp.bfloat16)
+    rotated = exact_dot(grad_ref[...] * sign, table) * (width**-0.5)
+    limit = column(4.0 * jnp.exp2(expo_ref[...].astype(jnp.float32)))
+    terms_ref[...] = jnp.clip(rotated, -limit, limit).astype(terms_ref.dtype)
+    own = pl.ds(pl.multiple_of(me_ref[0] * owned, owned), owned)
+    own_sign = (2 * bits_ref[own, :] - 1).astype(jnp.float32)
+    own_sign_ref[...] = own_sign * (width**-0.5 / replicas)
+    decayed_ref[...] = 0.9 * momentum_ref[...]
+
+
+def encode(me, grad, expo, bits, table, params, momentum):
+    shard, width = grad.shape
+    owned = params.shape[0]
+    f32 = jnp.float32
+    smem = pl.BlockSpec(memory_space=pltpu.SMEM)
+    vmem = pl.BlockSpec(memory_space=pltpu.VMEM)
+    hbm = pl.BlockSpec(memory_space=pltpu.HBM)
+    return pl.pallas_call(
+        encode_kernel,
+        out_shape=(
+            jax.ShapeDtypeStruct((shard, width), jnp.bfloat16),
+            jax.ShapeDtypeStruct((width, width), f32),
+            jax.ShapeDtypeStruct((owned, width), f32),
+            jax.ShapeDtypeStruct((owned, width), f32),
+            jax.ShapeDtypeStruct((owned, width), f32),
+        ),
+        in_specs=[smem] + [hbm] * 6,
+        out_specs=(vmem,) * 5,
+        scratch_shapes=[
+            pltpu.VMEM((shard, width), f32),
+            pltpu.VMEM((1, shard), jnp.int32),
+            pltpu.VMEM((shard, width), jnp.int32),
+            pltpu.VMEM((owned, width), f32),
+            pltpu.SemaphoreType.DMA((6,)),
+        ],
+        compiler_params=pltpu.CompilerParams(vmem_limit_bytes=4 * 2**20),
+    )(
+        me,
+        *(
+            pltpu.with_memory_space_constraint(value, pltpu.HBM)
+            for value in (grad, expo, bits, table, params, momentum)
+        ),
+    )
 
 
 def place_kernel(core_ref, mine_ref, other_ref, out_ref):
@@ -126,32 +178,23 @@
 
 
 def per_device(pseudo_grad, grad_expo, sign_bits, params, momentum, param_expo):
-    shard, width = sign_bits.shape
-    owned = params.shape[0]
+    owned, width = params.shape
     replicas = lax.axis_size(("zl", "c"))
-    table = jnp.asarray(hadamard(width), jnp.bfloat16)
-    vmem = pl.BlockSpec(memory_space=pltpu.VMEM)
-
-    terms = pl.pallas_call(
-        encode_kernel,
-        out_shape=jax.ShapeDtypeStruct((shard, width), jnp.bfloat16),
-        in_specs=[vmem] * 4,
-        out_specs=vmem,
-    )(pseudo_grad[0], grad_expo[0][:, None], sign_bits, table)
+    me = lax.axis_index(("zl", "c")).astype(jnp.int32)[None]
+    table = jnp.asarray(hadamard(width))
+    terms, table, params, decayed, own_sign = encode(
+        me, pseudo_grad[0], grad_expo, sign_bits, table, params, momentum
+    )
     terms = lax.all_to_all(terms, ("zl", "c"), split_axis=0, concat_axis=0, tiled=True)
 
-    me = lax.axis_index(("zl", "c"))
-    own_bits = lax.dynamic_slice_in_dim(sign_bits, me * owned, owned, 0)
-    new_params, new_momentum, codes = pl.pallas_call(
-        update_kernel,
-        out_shape=(
-            jax.ShapeDtypeStruct((owned, width), jnp.float32),
-            jax.ShapeDtypeStruct((owned, width), jnp.float32),
-            jax.ShapeDtypeStruct((owned, width), jnp.bfloat16),
-        ),
-        in_specs=[vmem] * 6,
-        out_specs=(vmem,) * 3,
-    )(terms.reshape(replicas, owned, width), own_bits, params, momentum, param_expo[:, None], table)
+    total = jnp.sum(terms.reshape(replicas, owned, width).astype(jnp.float32), axis=0)
+    delta = jnp.dot(total, table, precision=lax.Precision.HIGHEST) * own_sign
+    new_params = params - 0.7 * (delta + 0.9 * (decayed + delta))
+    inverse = jnp.exp2(-param_expo.astype(jnp.float32))[:, None]
+    codes = jnp.clip(new_params * inverse, -4.0, 4.0).astype(jnp.bfloat16)
+    codes, delta = lax.optimization_barrier((codes, delta))
+    new_momentum = decayed + delta
+    new_params = params - 0.7 * (delta + 0.9 * new_momentum)
 
     mine = gather(gather(codes, classes()), cubes())
     other = lax.ppermute(mine, "c", [(0, 1), (1, 0)])

time: 82 us -> 77.7 us (0.948)
  local copies, waits for them, and re-layouts: 5.51 us -> 0.15 us
  Pallas kernels: 6.16 us -> 4.46 us
  waiting for transfers between devices: 6.59 us -> 7.95 us
  other arithmetic: 0 us -> 1.29 us
    all_to_all x1, waiting for transfers between devices: 2.47 us -> 4.45 us  [per_device(): lax.all_to_all(terms, ('zl', 'c'), split_axis=0, concat_axis=0, tiled=True)]
    pallas_call x2 -> x1, Pallas kernels: 3.72 us -> 2.02 us  [encode(): pl.pallas_call(encode_kernel, out_shape=(jax.ShapeDtypeStruct((shard, wid...]
    another operation x1 -> x0, local copies, waits for them, and re-layouts: 1.39 us -> none  [per_device(): grad_expo[0][:, None]]
    broadcast_in_dim x1 -> x0, local copies, waits for them, and re-layouts: 1.33 us -> none  [per_device(): param_expo[:, None]]
    dynamic_slice x1 -> x0, local copies, waits for them, and re-layouts: 1.31 us -> none  [per_device(): own_bits = lax.dynamic_slice_in_dim(sign_bits, me * owned, owned, 0)]
  transfers between devices with their start and end apart: 2 -> 2, of which waited for: 2 -> 2; matrix products, arithmetic and copies ran while one was open for 3% -> 2% of each run, Pallas kernels for 0% -> 0%
where the time goes in v4:
time: 77.7 us; the launch traced here: 77.4 us
  blocking collectives  50.6 us (65%)
  starting transfers between devices  12.1 us (16%)
  waiting for transfers between devices  7.95 us (10%)
  Pallas kernels  4.46 us (6%)
  other arithmetic  1.29 us (2%)
    all_to_all x2, blocking collectives, gather(): lax.all_to_all(copies.reshape((-1,) + value.shape[1:]), AXES, split_axis=...  50.6 us
    all_to_all x1, starting transfers between devices, per_device(): lax.all_to_all(terms, ('zl', 'c'), split_axis=0, concat_axis=0, tiled=True)  10.1 us
    all_to_all x1, waiting for transfers between devices, per_device(): lax.all_to_all(terms, ('zl', 'c'), split_axis=0, concat_axis=0, tiled=True)  4.45 us
    ppermute x1, waiting for transfers between devices, per_device(): other = lax.ppermute(mine, 'c', [(0, 1), (1, 0)])  3.51 us
    pallas_call x1, Pallas kernels, place(): pl.pallas_call(place_kernel, out_shape=jax.ShapeDtypeStruct((4,) + block,...  2.44 us
    pallas_call x1, Pallas kernels, encode(): pl.pallas_call(encode_kernel, out_shape=(jax.ShapeDtypeStruct((shard, wid...  2.02 us
    ppermute x1, starting transfers between devices, per_device(): other = lax.ppermute(mine, 'c', [(0, 1), (1, 0)])  1.91 us
  transfers between devices with their start and end apart: 2, of which 2 were waited for; matrix products, arithmetic and copies ran while one was open for 2% of the time, Pallas kernels for 0%

profile of v4, /device:TPU:1, one launch (start us, length us, event | category | flops | bytes accessed | tf_op | source)
XLA Modules:
  0.0 77.4 jit_solution(11472890264203750768)
XLA Ops:
  0.6 2.0 %shard_map.94 = (bf16[128,256]{1,0:T(8,128)(2,1)}, f32[256,256]{1,0:T(8,128)S(1)}, f32[16,256]{1,0:T(8,128)S(1)}, f32[16,256]{1,0:T(8,128)S(1)}, f32[16,256]{1,0:T(8,128)S(1)}) custom-call(s32[1]{0:T(128)} %bitcast.me_ref, f32[128,256]{1,0:T(8,128)} %bitcast.16, s32[1,128]{1,0:T(1,128)} %expo_in.1, s32[128,256]{1,0:T(8,128)} %bits_in.1, ...), custom_call_target="tpu_custom_call" | custom-call | tf_op jit(solution)/shard_map/pallas_call | solution.py:118
  2.7 10.1 %all-to-all-start = ((bf16[8,16,256]{2,1,0:T(8,128)(2,1)}), bf16[8,16,256]{2,1,0:T(8,128)(2,1)S(1)}, u32[]{:S(2)}, u32[]{:S(2)}) async-start(bf16[8,16,256]{2,1,0:T(8,128)(2,1)} %bitcast.2), calls=%async_computation | async-start | bytes 131072 | tf_op jit(solution)/shard_map/all_to_all | solution.py:188
  12.8 0.7 multiply_exponential_fusion
  13.5 4.4 %all-to-all-done = bf16[8,16,256]{2,1,0:T(8,128)(2,1)S(1)} async-done(((bf16[8,16,256]{2,1,0:T(8,128)(2,1)}), bf16[8,16,256]{2,1,0:T(8,128)(2,1)S(1)}, u32[]{:S(2)}, u32[]{:S(2)}) %all-to-all-start) | async-done | bytes 65568 | tf_op jit(solution)/shard_map/all_to_all | solution.py:188
  17.9 0.2 clamp_convert_fusion
  18.2 28.9 %all_to_all.24 = bf16[32,16,256]{2,1,0:T(8,128)(2,1)S(1)} all-to-all(bf16[32,16,256]{2,1,0:T(8,128)(2,1)S(1)} %broadcast_in_dim.23), channel_id=1, replica_groups={{0,256,2,258,4,260,6,262,8,264,10,266,12,268,14,270,32,288,34,290,36,29..., dimensions={0} | all-to-all | bytes 524288 | tf_op jit(solution)/shard_map/all_to_all | solution.py:174
  47.1 0.1 broadcast_in_dim.25
  47.2 21.7 %all_to_all.25 = bf16[8,512,256]{2,1,0:T(8,128)(2,1)S(1)} all-to-all(bf16[8,512,256]{2,1,0:T(8,128)(2,1)S(1)} %broadcast_in_dim.25), channel_id=1, replica_groups={{0,128,1,129,16,144,17,145},{256,384,257,385,272,400,273,401},{8,136,9,..., dimensions={0} | all-to-all | bytes 4194304 | tf_op jit(solution)/shard_map/all_to_all | solution.py:174
  68.9 1.9 %collective-permute-start = (bf16[4096,256]{1,0:T(8,128)(2,1)S(1)}, bf16[4096,256]{1,0:T(8,128)(2,1)S(1)}, u32[]{:S(2)}, u32[]{:S(2)}) collective-permute-start(bf16[4096,256]{1,0:T(8,128)(2,1)S(1)} %bitcast.11), channel_id=1, source_target_pairs={{0,64},{64,0},{1,65},{65,1},{2,66},{66,2},{3,67},{67,3},{4,68},{68... | collective-permute-start | bytes 6291464 | tf_op jit(solution)/shard_map/ppermute | solution.py:200
  70.8 0.6 multiply_subtract_fusion
  71.5 3.5 %collective-permute-done = bf16[4096,256]{1,0:T(8,128)(2,1)S(1)} collective-permute-done((bf16[4096,256]{1,0:T(8,128)(2,1)S(1)}, bf16[4096,256]{1,0:T(8,128)(2,1)S(1)}, u32[]{:S(2)}, u32[]{:S(2)}) %collective-permute-start) | collective-permute-done | bytes 2097184 | tf_op jit(solution)/shard_map/ppermute | solution.py:200
  75.0 2.4 %shard_map.95 = bf16[4,2,4,2,2,2,2,16,256]{8,7,6,5,4,3,2,1,0:T(8,128)(2,1)} custom-call(s32[1]{0:T(128)} %bitcast.3.core_ref, bf16[2,2,2,2,2,4,2,16,256]{8,7,6,5,4,3,2,1,0:T(8,128)(2,1)S(1)} %bitcast.12, bf16[2,2,2,2,2,4,2,16,256]{8,7,6,5,4,3,2,1,0:T(8,128)(2,1)S(1)} %bitcast.13), custom_call_target="tpu_custom_call" | custom-call | bytes 8388608 | tf_op jit(solution)/shard_map/pallas_call | solution.py:159
  (2 shorter events, 0.0 us)
Async XLA Ops:
  2.7 15.2 %all-to-all-start = ((bf16[8,16,256]{2,1,0:T(8,128)(2,1)}), bf16[8,16,256]{2,1,0:T(8,128)(2,1)S(1)}, u32[]{:S(2)}, u32[]{:S(2)}) async-start(bf16[8,16,256]{2,1,0:T(8,128)(2,1)} %bitcast.2), calls=%async_computation | async-start | bytes 131072 | tf_op jit(solution)/shard_map/all_to_all | solution.py:188
  68.9 6.0 %collective-permute-start = (bf16[4096,256]{1,0:T(8,128)(2,1)S(1)}, bf16[4096,256]{1,0:T(8,128)(2,1)S(1)}, u32[]{:S(2)}, u32[]{:S(2)}) collective-permute-start(bf16[4096,256]{1,0:T(8,128)(2,1)S(1)} %bitcast.11), channel_id=1, source_target_pairs={{0,64},{64,0},{1,65},{65,1},{2,66},{66,2},{3,67},{67,3},{4,68},{68... | collective-permute-start | bytes 6291464 | tf_op jit(solution)/shard_map/ppermute | solution.py:200

commit v5 on v4

--- a/solution.py
+++ b/solution.py
@@ -9,7 +9,7 @@
 
 SIZES = (("zl", 4), ("c", 2), ("x", 4), ("zh", 2), ("y", 8))
 AXES = tuple(name for name, _ in SIZES)
-BITS = (0, 1)
+CLASSES = 4
 
 
 def device(x, y, z, core):
@@ -17,34 +17,35 @@
     return (((z % 4 * 2 + core) * 4 + x) * 2 + z // 4) * 8 + y
 
 
+def chips():
+    return [(x, y, z) for x in range(4) for y in range(8) for z in range(8)]
+
+
 def classes():
     return [
         [
-            device(2 * xh + px, 2 * yh + py, 4 * zh + 2 * zm + pz, core)
-            for xh in BITS
-            for zh in BITS
-            for yh in range(4)
-            for zm in BITS
+            device(kind - 2 * y - 3 * z, y, z, core)
+            for zh in range(2)
+            for y in range(8)
+            for z in range(4 * zh, 4 * zh + 4)
         ]
-        for px in BITS
-        for py in BITS
-        for pz in BITS
-        for core in BITS
-    ]
-
-
-def cubes():
+        for kind in range(CLASSES)
+        for core in (0, 1)
+    ]
+
+
+NEIGHBOURS = {
+    1: ((1, 0, 0), (0, 0, -1)),
+    2: ((0, 1, 0), (0, -1, 0)),
+    3: ((-1, 0, 0), (0, 0, 1)),
+}
+
+
+def from_neighbours(step):
     return [
-        [
-            device(2 * xh + way * px, 2 * yh + way * py, 2 * zm + way * pz, core)
-            for px in BITS
-            for py in BITS
-            for pz in BITS
-        ]
-        for core, way in ((0, 1), (1, -1))
-        for xh in range(2)
-        for yh in range(4)
-        for zm in range(4)
+        (device(x + dx, y + dy, z + dz, core), device(x, y, z, core))
+        for core, (dx, dy, dz) in enumerate(NEIGHBOURS[step])
+        for x, y, z in chips()
     ]
 
 
@@ -143,30 +144,34 @@
     )
 
 
-def place_kernel(core_ref, mine_ref, other_ref, out_ref):
-    x = pl.program_id(0)
-    core = core_ref[0]
-    for side, part_ref in ((core, mine_ref), (1 - core, other_ref)):
-        for py in BITS:
-            for pz in BITS:
-                out_ref[0, :, :, py, :, pz, side] = part_ref[x % 2, py, pz, x // 2]
-
-
-def place(core, mine, other):
-    owned, width = mine.shape[-2:]
-    block = (2, 4, 2, 2, 2, 2, owned, width)
+def place_kernel(spot_ref, *refs):
+    out_ref = refs[-1]
+    kind, core = spot_ref[0], spot_ref[1]
+    for step in range(CLASSES):
+        for side, part_ref in ((core, refs[step]), (1 - core, refs[CLASSES + step])):
+            for y in range(out_ref.shape[2]):
+                for z in range(out_ref.shape[3]):
+                    x = lax.rem(kind + step + 2 * y + z, 4)
+                    out_ref[x, 0, y, z, side] = part_ref[pl.program_id(0), y, z]
+
+
+def place(kind, core, mine, others):
+    width = mine[0].shape[-1]
+    parts = [part.reshape(4, 4, 4, -1, width) for part in (*mine, *others)]
+    owned = parts[0].shape[3]
+    block = (4, 1, 4, 4, 2, owned, width)
     vmem = pl.BlockSpec(memory_space=pltpu.VMEM)
     return pl.pallas_call(
         place_kernel,
-        out_shape=jax.ShapeDtypeStruct((4,) + block, mine.dtype),
+        out_shape=jax.ShapeDtypeStruct((4, 4, 4, 4, 2, owned, width), parts[0].dtype),
         grid=(4,),
-        in_specs=[pl.BlockSpec(memory_space=pltpu.SMEM), vmem, vmem],
-        out_specs=pl.BlockSpec((1,) + block, lambda x: (x,) + (0,) * len(block)),
+        in_specs=[pl.BlockSpec(memory_space=pltpu.SMEM)] + [vmem] * len(parts),
+        out_specs=pl.BlockSpec(block, lambda i: (0, i, 0, 0, 0, 0, 0)),
         cost_estimate=pl.CostEstimate(
-            flops=0, bytes_accessed=8 * mine.size, transcendentals=0
+            flops=0, bytes_accessed=32 * parts[0].size, transcendentals=0
         ),
         compiler_params=pltpu.CompilerParams(vmem_limit_bytes=16 * 2**20),
-    )(core, mine, other)
+    )(jnp.stack([kind, core]), *parts)
 
 
 def gather(value, groups):
@@ -196,11 +201,13 @@
     new_momentum = decayed + delta
     new_params = params - 0.7 * (delta + 0.9 * new_momentum)
 
-    mine = gather(gather(codes, classes()), cubes())
-    other = lax.ppermute(mine, "c", [(0, 1), (1, 0)])
-    parts = (2, 2, 2, 2, 2, 4, 2, owned, width)
-    core = lax.axis_index("c").astype(jnp.int32)[None]
-    whole = place(core, mine.reshape(parts), other.reshape(parts))
+    own = gather(codes, classes())
+    mine = [own] + [
+        lax.ppermute(own, AXES, from_neighbours(step)) for step in range(1, CLASSES)
+    ]
+    others = [lax.ppermute(part, "c", [(0, 1), (1, 0)]) for part in mine]
+    x, y, zl, core = (lax.axis_index(name) for name in ("x", "y", "zl", "c"))
+    whole = place(lax.rem(x + 2 * y + 3 * zl, CLASSES), core, mine, others)
     return new_params, new_momentum, whole.reshape(-1, width)
 
 

time: 77.7 us -> 78.3 us (level)
  starting transfers between devices: 12.1 us -> 31.8 us
  blocking collectives: 50.6 us -> 32.4 us
  waiting for transfers between devices: 7.95 us -> 5.39 us
  Pallas kernels: 4.46 us -> 5.72 us
    ppermute x1 -> x7, starting transfers between devices: 1.91 us -> 21.7 us  [the longest x4 13 us: per_device(): others = [lax.ppermute(part, 'c', [(0, 1), (1, 0)]) for part in mine]]
    all_to_all x2 -> x1, blocking collectives: 50.6 us -> 32.4 us  [gather(): lax.all_to_all(copies.reshape((-1,) + value.shape[1:]), AXES, split_axis=...]
    ppermute x1 -> x7, waiting for transfers between devices: 3.51 us -> 0.95 us  [the longest x4 0.94 us: per_device(): others = [lax.ppermute(part, 'c', [(0, 1), (1, 0)]) for part in mine]]
    pallas_call x1, Pallas kernels: 2.44 us -> 3.71 us  [place(): pl.pallas_call(place_kernel, out_shape=jax.ShapeDtypeStruct((4, 4, 4, 4,...]
  transfers between devices with their start and end apart: 2 -> 8, of which waited for: 2 -> 2; matrix products, arithmetic and copies ran while one was open for 2% -> 2% of each run, Pallas kernels for 0% -> 0%
where the time goes in v5:
time: 78.3 us; the launch traced here: 77.7 us
  blocking collectives  32.4 us (41%)
  starting transfers between devices  31.8 us (41%)
  Pallas kernels  5.72 us (7%)
  waiting for transfers between devices  5.39 us (7%)
  other arithmetic  1.37 us (2%)
    all_to_all x1, blocking collectives, gather(): lax.all_to_all(copies.reshape((-1,) + value.shape[1:]), AXES, split_axis=...  32.4 us
    ppermute x4, starting transfers between devices, per_device(): others = [lax.ppermute(part, 'c', [(0, 1), (1, 0)]) for part in mine]  13 us
    all_to_all x1, starting transfers between devices, per_device(): lax.all_to_all(terms, ('zl', 'c'), split_axis=0, concat_axis=0, tiled=True)  10.1 us
    ppermute x3, starting transfers between devices, per_device(): lax.ppermute(own, AXES, from_neighbours(step))  8.66 us
    all_to_all x1, waiting for transfers between devices, per_device(): lax.all_to_all(terms, ('zl', 'c'), split_axis=0, concat_axis=0, tiled=True)  4.45 us
    pallas_call x1, Pallas kernels, place(): pl.pallas_call(place_kernel, out_shape=jax.ShapeDtypeStruct((4, 4, 4, 4,...  3.71 us
    pallas_call x1, Pallas kernels, encode(): pl.pallas_call(encode_kernel, out_shape=(jax.ShapeDtypeStruct((shard, wid...  2.02 us
  transfers between devices with their start and end apart: 8, of which 2 were waited for; matrix products, arithmetic and copies ran while one was open for 2% of the time, Pallas kernels for 0%

profile of v5, /device:TPU:1, one launch (start us, length us, event | category | flops | bytes accessed | tf_op | source)
XLA Modules:
  0.0 77.7 jit_solution(13195075836335513780)
XLA Ops:
  0.6 2.0 %shard_map.94 = (bf16[128,256]{1,0:T(8,128)(2,1)}, f32[256,256]{1,0:T(8,128)S(1)}, f32[16,256]{1,0:T(8,128)S(1)}, f32[16,256]{1,0:T(8,128)S(1)}, f32[16,256]{1,0:T(8,128)S(1)}) custom-call(s32[1]{0:T(128)} %bitcast.me_ref, f32[128,256]{1,0:T(8,128)} %bitcast.28, s32[1,128]{1,0:T(1,128)} %expo_in.1, s32[128,256]{1,0:T(8,128)} %bits_in.1, ...), custom_call_target="tpu_custom_call" | custom-call | tf_op jit(solution)/shard_map/pallas_call | solution.py:119
  2.7 10.1 %all-to-all-start = ((bf16[8,16,256]{2,1,0:T(8,128)(2,1)}), bf16[8,16,256]{2,1,0:T(8,128)(2,1)S(1)}, u32[]{:S(2)}, u32[]{:S(2)}) async-start(bf16[8,16,256]{2,1,0:T(8,128)(2,1)} %bitcast.2), calls=%async_computation | async-start | bytes 131072 | tf_op jit(solution)/shard_map/all_to_all | solution.py:193
  12.8 0.7 multiply_exponential_fusion
  13.5 4.4 %all-to-all-done = bf16[8,16,256]{2,1,0:T(8,128)(2,1)S(1)} async-done(((bf16[8,16,256]{2,1,0:T(8,128)(2,1)}), bf16[8,16,256]{2,1,0:T(8,128)(2,1)S(1)}, u32[]{:S(2)}, u32[]{:S(2)}) %all-to-all-start) | async-done | bytes 65568 | tf_op jit(solution)/shard_map/all_to_all | solution.py:193
  17.9 0.2 clamp_convert_fusion
  18.2 32.4 %all_to_all.18 = bf16[64,16,256]{2,1,0:T(8,128)(2,1)S(1)} all-to-all(bf16[64,16,256]{2,1,0:T(8,128)(2,1)S(1)} %broadcast_in_dim.5), channel_id=1, replica_groups={{0,144,288,432,33,177,257,401,2,146,290,434,35,179,259,403,4,148,292,43..., dimensions={0} | all-to-all | bytes 1048576 | tf_op jit(solution)/shard_map/all_to_all | solution.py:179
  50.6 2.9 %collective-permute-start.2 = (bf16[1024,256]{1,0:T(8,128)(2,1)S(1)}, bf16[1024,256]{1,0:T(8,128)(2,1)S(1)}, u32[]{:S(2)}, u32[]{:S(2)}) collective-permute-start(bf16[1024,256]{1,0:T(8,128)(2,1)S(1)} %bitcast.17), channel_id=1, source_target_pairs={{48,0},{176,128},{304,256},{432,384},{56,8},{184,136},{312,264},{4... | collective-permute-start | bytes 1572872 | tf_op jit(solution)/shard_map/ppermute | solution.py:206
  53.5 2.0 %collective-permute-start.1 = (bf16[1024,256]{1,0:T(8,128)(2,1)S(1)}, bf16[1024,256]{1,0:T(8,128)(2,1)S(1)}, u32[]{:S(2)}, u32[]{:S(2)}) collective-permute-start(bf16[1024,256]{1,0:T(8,128)(2,1)S(1)} %bitcast.18), channel_id=1, source_target_pairs={{1,0},{129,128},{257,256},{385,384},{9,8},{137,136},{265,264},{393... | collective-permute-start | bytes 1572872 | tf_op jit(solution)/shard_map/ppermute | solution.py:206
  55.5 3.8 %collective-permute-start = (bf16[1024,256]{1,0:T(8,128)(2,1)S(1)}, bf16[1024,256]{1,0:T(8,128)(2,1)S(1)}, u32[]{:S(2)}, u32[]{:S(2)}) collective-permute-start(bf16[1024,256]{1,0:T(8,128)(2,1)S(1)} %bitcast.19), channel_id=1, source_target_pairs={{16,0},{144,128},{272,256},{400,384},{24,8},{152,136},{280,264},{4... | collective-permute-start | bytes 1572872 | tf_op jit(solution)/shard_map/ppermute | solution.py:206
  59.3 6.4 %collective-permute-start.3 = (bf16[1024,256]{1,0:T(8,128)(2,1)S(1)}, bf16[1024,256]{1,0:T(8,128)(2,1)S(1)}, u32[]{:S(2)}, u32[]{:S(2)}) collective-permute-start(bf16[1024,256]{1,0:T(8,128)(2,1)S(1)} %bitcast.20), channel_id=1, source_target_pairs={{0,64},{64,0},{1,65},{65,1},{2,66},{66,2},{3,67},{67,3},{4,68},{68... | collective-permute-start | bytes 1572872 | tf_op jit(solution)/shard_map/ppermute | solution.py:208
  65.7 0.0 collective-permute-done.2
  65.7 1.9 %collective-permute-start.6 = (bf16[1024,256]{1,0:T(8,128)(2,1)S(1)}, bf16[1024,256]{1,0:T(8,128)(2,1)S(1)}, u32[]{:S(2)}, u32[]{:S(2)}) collective-permute-start(bf16[1024,256]{1,0:T(8,128)(2,1)S(1)} %collective-permute-done.2), channel_id=1, source_target_pairs={{0,64},{64,0},{1,65},{65,1},{2,66},{66,2},{3,67},{67,3},{4,68},{68... | collective-permute-start | bytes 1572872 | tf_op jit(solution)/shard_map/ppermute | solution.py:208
  67.6 0.0 collective-permute-done.1
  67.6 2.4 %collective-permute-start.5 = (bf16[1024,256]{1,0:T(8,128)(2,1)S(1)}, bf16[1024,256]{1,0:T(8,128)(2,1)}, u32[]{:S(2)}, u32[]{:S(2)}) collective-permute-start(bf16[1024,256]{1,0:T(8,128)(2,1)S(1)} %collective-permute-done.1), channel_id=1, source_target_pairs={{0,64},{64,0},{1,65},{65,1},{2,66},{66,2},{3,67},{67,3},{4,68},{68... | collective-permute-start | bytes 1572872 | tf_op jit(solution)/shard_map/ppermute | solution.py:208
  70.0 0.0 collective-permute-done
  70.1 2.3 %collective-permute-start.4 = (bf16[1024,256]{1,0:T(8,128)(2,1)S(1)}, bf16[1024,256]{1,0:T(8,128)(2,1)}, u32[]{:S(2)}, u32[]{:S(2)}) collective-permute-start(bf16[1024,256]{1,0:T(8,128)(2,1)S(1)} %collective-permute-done), channel_id=1, source_target_pairs={{0,64},{64,0},{1,65},{65,1},{2,66},{66,2},{3,67},{67,3},{4,68},{68... | collective-permute-start | bytes 1572872 | tf_op jit(solution)/shard_map/ppermute | solution.py:208
  72.4 0.1 pad_add_fusion.spot_ref
  72.4 0.6 multiply_subtract_fusion
  73.0 0.0 collective-permute-done.3
  73.1 0.0 collective-permute-done.6
  73.1 0.0 collective-permute-done.5
  73.1 0.9 %collective-permute-done.4 = bf16[1024,256]{1,0:T(8,128)(2,1)} collective-permute-done((bf16[1024,256]{1,0:T(8,128)(2,1)S(1)}, bf16[1024,256]{1,0:T(8,128)(2,1)}, u32[]{:S(2)}, u32[]{:S(2)}) %collective-permute-start.4) | collective-permute-done | bytes 524320 | tf_op jit(solution)/shard_map/ppermute | solution.py:208
  74.0 3.7 %shard_map.95 = bf16[4,4,4,4,2,16,256]{6,5,4,3,2,1,0:T(8,128)(2,1)} custom-call(s32[2]{0:T(128)S(1)} %pad_add_fusion.spot_ref, bf16[4,4,4,16,256]{4,3,2,1,0:T(8,128)(2,1)S(1)} %bitcast.21, bf16[4,4,4,16,256]{4,3,2,1,0:T(8,128)(2,1)S(1)} %bitcast.24, bf16[4,4,4,16,256]{4,3,2,1,0:T(8,128)(2,1)S(1)} %bitcast.23, bf16[4,4,4,16,256]{4,3,2,1,0:T(8,128)(2,1)S(1)} %bitcast.22, ...), custom_call_target="tpu_custom_call" | custom-call | bytes 8388608 | tf_op jit(solution)/shard_map/pallas_call | solution.py:164
  (2 shorter events, 0.0 us)
Async XLA Ops:
  2.7 15.2 %all-to-all-start = ((bf16[8,16,256]{2,1,0:T(8,128)(2,1)}), bf16[8,16,256]{2,1,0:T(8,128)(2,1)S(1)}, u32[]{:S(2)}, u32[]{:S(2)}) async-start(bf16[8,16,256]{2,1,0:T(8,128)(2,1)} %bitcast.2), calls=%async_computation | async-start | bytes 131072 | tf_op jit(solution)/shard_map/all_to_all | solution.py:193
  50.6 15.1 %collective-permute-start.2 = (bf16[1024,256]{1,0:T(8,128)(2,1)S(1)}, bf16[1024,256]{1,0:T(8,128)(2,1)S(1)}, u32[]{:S(2)}, u32[]{:S(2)}) collective-permute-start(bf16[1024,256]{1,0:T(8,128)(2,1)S(1)} %bitcast.17), channel_id=1, source_target_pairs={{48,0},{176,128},{304,256},{432,384},{56,8},{184,136},{312,264},{4... | collective-permute-start | bytes 1572872 | tf_op jit(solution)/shard_map/ppermute | solution.py:206
  53.5 14.1 %collective-permute-start.1 = (bf16[1024,256]{1,0:T(8,128)(2,1)S(1)}, bf16[1024,256]{1,0:T(8,128)(2,1)S(1)}, u32[]{:S(2)}, u32[]{:S(2)}) collective-permute-start(bf16[1024,256]{1,0:T(8,128)(2,1)S(1)} %bitcast.18), channel_id=1, source_target_pairs={{1,0},{129,128},{257,256},{385,384},{9,8},{137,136},{265,264},{393... | collective-permute-start | bytes 1572872 | tf_op jit(solution)/shard_map/ppermute | solution.py:206
  55.5 14.6 %collective-permute-start = (bf16[1024,256]{1,0:T(8,128)(2,1)S(1)}, bf16[1024,256]{1,0:T(8,128)(2,1)S(1)}, u32[]{:S(2)}, u32[]{:S(2)}) collective-permute-start(bf16[1024,256]{1,0:T(8,128)(2,1)S(1)} %bitcast.19), channel_id=1, source_target_pairs={{16,0},{144,128},{272,256},{400,384},{24,8},{152,136},{280,264},{4... | collective-permute-start | bytes 1572872 | tf_op jit(solution)/shard_map/ppermute | solution.py:206
  59.3 13.8 %collective-permute-start.3 = (bf16[1024,256]{1,0:T(8,128)(2,1)S(1)}, bf16[1024,256]{1,0:T(8,128)(2,1)S(1)}, u32[]{:S(2)}, u32[]{:S(2)}) collective-permute-start(bf16[1024,256]{1,0:T(8,128)(2,1)S(1)} %bitcast.20), channel_id=1, source_target_pairs={{0,64},{64,0},{1,65},{65,1},{2,66},{66,2},{3,67},{67,3},{4,68},{68... | collective-permute-start | bytes 1572872 | tf_op jit(solution)/shard_map/ppermute | solution.py:208
  65.7 7.4 %collective-permute-start.6 = (bf16[1024,256]{1,0:T(8,128)(2,1)S(1)}, bf16[1024,256]{1,0:T(8,128)(2,1)S(1)}, u32[]{:S(2)}, u32[]{:S(2)}) collective-permute-start(bf16[1024,256]{1,0:T(8,128)(2,1)S(1)} %collective-permute-done.2), channel_id=1, source_target_pairs={{0,64},{64,0},{1,65},{65,1},{2,66},{66,2},{3,67},{67,3},{4,68},{68... | collective-permute-start | bytes 1572872 | tf_op jit(solution)/shard_map/ppermute | solution.py:208
  67.6 5.4 %collective-permute-start.5 = (bf16[1024,256]{1,0:T(8,128)(2,1)S(1)}, bf16[1024,256]{1,0:T(8,128)(2,1)}, u32[]{:S(2)}, u32[]{:S(2)}) collective-permute-start(bf16[1024,256]{1,0:T(8,128)(2,1)S(1)} %collective-permute-done.1), channel_id=1, source_target_pairs={{0,64},{64,0},{1,65},{65,1},{2,66},{66,2},{3,67},{67,3},{4,68},{68... | collective-permute-start | bytes 1572872 | tf_op jit(solution)/shard_map/ppermute | solution.py:208
  70.1 3.9 %collective-permute-start.4 = (bf16[1024,256]{1,0:T(8,128)(2,1)S(1)}, bf16[1024,256]{1,0:T(8,128)(2,1)}, u32[]{:S(2)}, u32[]{:S(2)}) collective-permute-start(bf16[1024,256]{1,0:T(8,128)(2,1)S(1)} %collective-permute-done), channel_id=1, source_target_pairs={{0,64},{64,0},{1,65},{65,1},{2,66},{66,2},{3,67},{67,3},{4,68},{68... | collective-permute-start | bytes 1572872 | tf_op jit(solution)/shard_map/ppermute | solution.py:208

commit v6 on v4

--- a/solution.py
+++ b/solution.py
@@ -20,32 +20,36 @@
 def classes():
     return [
         [
-            device(2 * xh + px, 2 * yh + py, 4 * zh + 2 * zm + pz, core)
-            for xh in BITS
-            for zh in BITS
+            device(row + 2 * z, 2 * yh + (side + z) % 2, z, core)
+            for z in range(8)
             for yh in range(4)
-            for zm in BITS
         ]
-        for px in BITS
-        for py in BITS
-        for pz in BITS
+        for row in range(4)
+        for side in BITS
         for core in BITS
     ]
 
 
 def cubes():
-    return [
-        [
-            device(2 * xh + way * px, 2 * yh + way * py, 2 * zm + way * pz, core)
-            for px in BITS
-            for py in BITS
-            for pz in BITS
-        ]
-        for core, way in ((0, 1), (1, -1))
-        for xh in range(2)
-        for yh in range(4)
-        for zm in range(4)
-    ]
+    def place_of(chip):
+        x, y, z = chip
+        row = (x + 2 * z) % 4
+        return row % 2, row // 2, (y + z) % 2
+
+    groups = []
+    for core in BITS:
+        for x in range(core, 4, 2):
+            for y in range(core, 8, 2):
+                for z in range(core, 8, 2):
+                    cube = [
+                        ((x + i) % 4, (y + j) % 8, (z + k) % 8)
+                        for i in BITS
+                        for j in BITS
+                        for k in BITS
+                    ]
+                    cube.sort(key=place_of)
+                    groups.append([device(*chip, core) for chip in cube])
+    return groups
 
 
 def hadamard(width):
@@ -76,8 +80,9 @@
 
 
 def encode_kernel(me_ref, grad_in, expo_in, bits_in, table_in, params_in, momentum_in,
-                  terms_ref, table_ref, params_ref, decayed_ref, own_sign_ref,
-                  grad_ref, expo_ref, bits_ref, momentum_ref, sems):
+                  param_expo_in, terms_ref, table_ref, params_ref, decayed_ref,
+                  own_sign_ref, inverse_ref, grad_ref, expo_ref, bits_ref, momentum_ref,
+                  param_expo_ref, sems):
     inward = (
         (grad_in, grad_ref),
         (expo_in, expo_ref),
@@ -85,6 +90,7 @@
         (table_in, table_ref),
         (params_in, params_ref),
         (momentum_in, momentum_ref),
+        (param_expo_in, param_expo_ref),
     )
     copies = [
         pltpu.make_async_copy(source, target, sems.at[i])
@@ -106,9 +112,11 @@
     own_sign = (2 * bits_ref[own, :] - 1).astype(jnp.float32)
     own_sign_ref[...] = own_sign * (width**-0.5 / replicas)
     decayed_ref[...] = 0.9 * momentum_ref[...]
-
-
-def encode(me, grad, expo, bits, table, params, momentum):
+    inverse = column(jnp.exp2(-param_expo_ref[...].astype(jnp.float32)))
+    inverse_ref[...] = jnp.broadcast_to(inverse, inverse_ref.shape)
+
+
+def encode(me, grad, expo, bits, table, params, momentum, param_expo):
     shard, width = grad.shape
     owned = params.shape[0]
     f32 = jnp.float32
@@ -123,50 +131,87 @@
             jax.ShapeDtypeStruct((owned, width), f32),
             jax.ShapeDtypeStruct((owned, width), f32),
             jax.ShapeDtypeStruct((owned, width), f32),
+            jax.ShapeDtypeStruct((owned, width), f32),
         ),
-        in_specs=[smem] + [hbm] * 6,
-        out_specs=(vmem,) * 5,
+        in_specs=[smem] + [hbm] * 7,
+        out_specs=(vmem,) * 6,
         scratch_shapes=[
             pltpu.VMEM((shard, width), f32),
             pltpu.VMEM((1, shard), jnp.int32),
             pltpu.VMEM((shard, width), jnp.int32),
             pltpu.VMEM((owned, width), f32),
-            pltpu.SemaphoreType.DMA((6,)),
+            pltpu.VMEM((1, owned), jnp.int32),
+            pltpu.SemaphoreType.DMA((7,)),
         ],
         compiler_params=pltpu.CompilerParams(vmem_limit_bytes=4 * 2**20),
     )(
         me,
         *(
             pltpu.with_memory_space_constraint(value, pltpu.HBM)
-            for value in (grad, expo, bits, table, params, momentum)
+            for value in (grad, expo, bits, table, params, momentum, param_expo)
         ),
     )
 
 
-def place_kernel(core_ref, mine_ref, other_ref, out_ref):
-    x = pl.program_id(0)
+def fill(core_ref, mine_ref, other_ref, out_ref):
+    xh = pl.program_id(0)
     core = core_ref[0]
     for side, part_ref in ((core, mine_ref), (1 - core, other_ref)):
-        for py in BITS:
-            for pz in BITS:
-                out_ref[0, :, :, py, :, pz, side] = part_ref[x % 2, py, pz, x // 2]
-
-
-def place(core, mine, other):
+        for zl in range(4):
+            half = xh if zl % 2 == 0 else 1 - xh
+            for py in BITS:
+                for zh in BITS:
+                    out_ref[0, 0, zh, :, py, zl, side] = part_ref[
+                        half, (py + zl) % 2, 4 * zh + zl
+                    ]
+
+
+def place_even_kernel(core_ref, mine_ref, other_ref, params_ref, decayed_ref, delta_ref,
+                      out_ref, new_params_ref, new_momentum_ref):
+    fill(core_ref, mine_ref, other_ref, out_ref)
+    delta = delta_ref[...]
+    new_momentum = decayed_ref[...] + delta
+    new_momentum_ref[...] = new_momentum
+    new_params_ref[...] = params_ref[...] - 0.7 * (delta + 0.9 * new_momentum)
+
+
+def place_odd_kernel(core_ref, mine_ref, other_ref, even_ref, out_ref):
+    fill(core_ref, mine_ref, other_ref, out_ref)
+
+
+def place(core, mine, other, owner=None, even=None):
     owned, width = mine.shape[-2:]
-    block = (2, 4, 2, 2, 2, 2, owned, width)
+    px = 0 if even is None else 1
+    block = (2, 4, 2, 4, 2, owned, width)
+    smem = pl.BlockSpec(memory_space=pltpu.SMEM)
     vmem = pl.BlockSpec(memory_space=pltpu.VMEM)
-    return pl.pallas_call(
-        place_kernel,
-        out_shape=jax.ShapeDtypeStruct((4,) + block, mine.dtype),
-        grid=(4,),
-        in_specs=[pl.BlockSpec(memory_space=pltpu.SMEM), vmem, vmem],
-        out_specs=pl.BlockSpec((1,) + block, lambda x: (x,) + (0,) * len(block)),
+    whole = jax.ShapeDtypeStruct((2, 2) + block, mine.dtype)
+    whole_spec = pl.BlockSpec((1, 1) + block, lambda xh: (xh, px) + (0,) * len(block))
+    small = jax.ShapeDtypeStruct((owned, width), jnp.float32)
+    small_spec = pl.BlockSpec((owned, width), lambda xh: (0, 0))
+    common = dict(
+        grid=(2,),
         cost_estimate=pl.CostEstimate(
             flops=0, bytes_accessed=8 * mine.size, transcendentals=0
         ),
         compiler_params=pltpu.CompilerParams(vmem_limit_bytes=16 * 2**20),
-    )(core, mine, other)
+    )
+    if even is None:
+        return pl.pallas_call(
+            place_even_kernel,
+            out_shape=(whole, small, small),
+            in_specs=[smem] + [vmem] * 5,
+            out_specs=(whole_spec, small_spec, small_spec),
+            **common,
+        )(core, mine, other, *owner)
+    return pl.pallas_call(
+        place_odd_kernel,
+        out_shape=whole,
+        in_specs=[smem, vmem, vmem, pl.BlockSpec(memory_space=pl.ANY)],
+        out_specs=whole_spec,
+        input_output_aliases={3: 0},
+        **common,
+    )(core, mine, other, even)
 
 
 def gather(value, groups):
@@ -182,25 +227,25 @@
     replicas = lax.axis_size(("zl", "c"))
     me = lax.axis_index(("zl", "c")).astype(jnp.int32)[None]
     table = jnp.asarray(hadamard(width))
-    terms, table, params, decayed, own_sign = encode(
-        me, pseudo_grad[0], grad_expo, sign_bits, table, params, momentum
+    terms, table, params, decayed, own_sign, inverse = encode(
+        me, pseudo_grad[0], grad_expo, sign_bits, table, params, momentum, param_expo[None]
     )
     terms = lax.all_to_all(terms, ("zl", "c"), split_axis=0, concat_axis=0, tiled=True)
 
     total = jnp.sum(terms.reshape(replicas, owned, width).astype(jnp.float32), axis=0)
     delta = jnp.dot(total, table, precision=lax.Precision.HIGHEST) * own_sign
     new_params = params - 0.7 * (delta + 0.9 * (decayed + delta))
-    inverse = jnp.exp2(-param_expo.astype(jnp.float32))[:, None]
     codes = jnp.clip(new_params * inverse, -4.0, 4.0).astype(jnp.bfloat16)
-    codes, delta = lax.optimization_barrier((codes, delta))
-    new_momentum = decayed + delta
-    new_params = params - 0.7 * (delta + 0.9 * new_momentum)
-
     mine = gather(gather(codes, classes()), cubes())
-    other = lax.ppermute(mine, "c", [(0, 1), (1, 0)])
-    parts = (2, 2, 2, 2, 2, 4, 2, owned, width)
+    halves = [
+        half.reshape(2, 2, 8, 4, owned, width) for half in jnp.split(mine, 2)
+    ]
+    others = [lax.ppermute(half, "c", [(0, 1), (1, 0)]) for half in halves]
     core = lax.axis_index("c").astype(jnp.int32)[None]
-    whole = place(core, mine.reshape(parts), other.reshape(parts))
+    whole, new_params, new_momentum = place(
+        core, halves[0], others[0], owner=(params, decayed, delta)
+    )
+    whole = place(core, halves[1], others[1], even=whole)
     return new_params, new_momentum, whole.reshape(-1, width)
 
 

time: 77.7 us -> 75.8 us (0.976)
  blocking collectives: 50.6 us -> 64.8 us
  starting transfers between devices: 12.1 us -> 4.33 us
  waiting for transfers between devices: 7.95 us -> 0.86 us
  other arithmetic: 1.29 us -> 0.01 us
    all_to_all x0 -> x1, blocking collectives: none -> 14.3 us  [per_device(): lax.all_to_all(terms, ('zl', 'c'), split_axis=0, concat_axis=0, tiled=True)]
    all_to_all x1 -> x0, starting transfers between devices: 10.1 us -> none  [per_device(): lax.all_to_all(terms, ('zl', 'c'), split_axis=0, concat_axis=0, tiled=True)]
    all_to_all x1 -> x0, waiting for transfers between devices: 4.45 us -> none  [per_device(): lax.all_to_all(terms, ('zl', 'c'), split_axis=0, concat_axis=0, tiled=True)]
    ppermute x1 -> x2, waiting for transfers between devices: 3.51 us -> 0.86 us  [per_device(): others = [lax.ppermute(half, 'c', [(0, 1), (1, 0)]) for half in halves]]
    ppermute x1 -> x2, starting transfers between devices: 1.91 us -> 4.33 us  [per_device(): others = [lax.ppermute(half, 'c', [(0, 1), (1, 0)]) for half in halves]]
    pallas_call x1 -> x2, Pallas kernels: 2.44 us -> 2.8 us  [the longest x1 1.4 us: place(): pl.pallas_call(place_even_kernel, out_shape=(whole, small, small), in_spe...]
  transfers between devices with their start and end apart: 2 -> 2, of which waited for: 2 -> 2; matrix products, arithmetic and copies ran while one was open for 2% -> 0% of each run, Pallas kernels for 0% -> 2%
where the time goes in v6:
time: 75.8 us; the launch traced here: 75.5 us
  blocking collectives  64.8 us (85%)
  starting transfers between devices  4.33 us (6%)
  Pallas kernels  4.2 us (6%)
  waiting for transfers between devices  0.86 us (1%)
    all_to_all x2, blocking collectives, gather(): lax.all_to_all(copies.reshape((-1,) + value.shape[1:]), AXES, split_axis=...  50.5 us
    all_to_all x1, blocking collectives, per_device(): lax.all_to_all(terms, ('zl', 'c'), split_axis=0, concat_axis=0, tiled=True)  14.3 us
    ppermute x2, starting transfers between devices, per_device(): others = [lax.ppermute(half, 'c', [(0, 1), (1, 0)]) for half in halves]  4.33 us
  transfers between devices with their start and end apart: 2, of which 2 were waited for; matrix products, arithmetic and copies ran while one was open for 0% of the time, Pallas kernels for 2%

profile of v6, /device:TPU:1, one launch (start us, length us, event | category | flops | bytes accessed | tf_op | source)
XLA Modules:
  0.0 75.5 jit_solution(1614515944095646288)
XLA Ops:
  0.6 1.4 %shard_map.94 = (bf16[128,256]{1,0:T(8,128)(2,1)S(1)}, f32[256,256]{1,0:T(8,128)S(1)}, f32[16,256]{1,0:T(8,128)S(1)}, f32[16,256]{1,0:T(8,128)S(1)}, f32[16,256]{1,0:T(8,128)S(1)}, /*index=5*/f32[16,256]{1,0:T(8,128)S(1)}) custom-call(s32[1]{0:T(128)} %bitcast.1.me_ref, f32[128,256]{1,0:T(8,128)} %bitcast.18, s32[1,128]{1,0:T(1,128)} %expo_in.1, ...), custom_call_target="tpu_custom_call" | custom-call | tf_op jit(solution)/shard_map/pallas_call | solution.py:126
  2.1 14.3 %all_to_all.21 = bf16[8,16,256]{2,1,0:T(8,128)(2,1)S(1)} all-to-all(bf16[8,16,256]{2,1,0:T(8,128)(2,1)S(1)} %bitcast.15), channel_id=1, replica_groups=mesh['zl'=4,'c'=2,'x'=4,'zh'=2,'y'=8] {'zl','c'}, dimensions={0} | all-to-all | bytes 131072 | tf_op jit(solution)/shard_map/all_to_all | solution.py:233
  16.4 0.2 clamp_convert_fusion
  16.7 25.8 %all_to_all.22 = bf16[32,16,256]{2,1,0:T(8,128)(2,1)S(1)} all-to-all(bf16[32,16,256]{2,1,0:T(8,128)(2,1)S(1)} %broadcast_in_dim.26), channel_id=1, replica_groups={{0,2,4,6,161,163,165,167,256,258,260,262,417,419,421,423,8,10,12,14,169..., dimensions={0} | all-to-all | bytes 524288 | tf_op jit(solution)/shard_map/all_to_all | solution.py:219
  42.5 0.1 broadcast_in_dim.28
  42.6 24.7 %all_to_all.23 = bf16[8,512,256]{2,1,0:T(8,128)(2,1)S(1)} all-to-all(bf16[8,512,256]{2,1,0:T(8,128)(2,1)S(1)} %broadcast_in_dim.28), channel_id=1, replica_groups={{0,1,129,128,16,17,145,144},{256,257,385,384,272,273,401,400},{8,9,137,..., dimensions={0} | all-to-all | bytes 4194304 | tf_op jit(solution)/shard_map/all_to_all | solution.py:219
  67.3 0.1 fusion
  67.5 1.9 %collective-permute-start = (bf16[2,2,8,4,16,256]{5,4,3,2,1,0:T(8,128)(2,1)S(1)}, bf16[2,2,8,4,16,256]{5,4,3,2,1,0:T(8,128)(2,1)S(1)}, u32[]{:S(2)}, u32[]{:S(2)}) collective-permute-start(bf16[2,2,8,4,16,256]{5,4,3,2,1,0:T(8,128)(2,1)S(1)} %bitcast.11), channel_id=1, source_target_pairs={{0,64},{64,0},{1,65},{65,1},{2,66},{66,2},{3,67},{67,3},{4,68},{68... | collective-permute-start | bytes 3145736 | tf_op jit(solution)/shard_map/ppermute | solution.py:243
  69.4 2.4 %collective-permute-start.1 = (bf16[2,2,8,4,16,256]{5,4,3,2,1,0:T(8,128)(2,1)S(1)}, bf16[2,2,8,4,16,256]{5,4,3,2,1,0:T(8,128)(2,1)S(1)}, u32[]{:S(2)}, u32[]{:S(2)}) collective-permute-start(bf16[2,2,8,4,16,256]{5,4,3,2,1,0:T(8,128)(2,1)S(1)} %bitcast.13), channel_id=1, source_target_pairs={{0,64},{64,0},{1,65},{65,1},{2,66},{66,2},{3,67},{67,3},{4,68},{68... | collective-permute-start | bytes 3145736 | tf_op jit(solution)/shard_map/ppermute | solution.py:243
  71.8 0.2 collective-permute-done.other_ref
  72.0 1.4 %shard_map.95 = (bf16[2,2,2,4,2,4,2,16,256]{8,7,6,5,4,3,2,1,0:T(8,128)(2,1)}, f32[16,256]{1,0:T(8,128)}, f32[16,256]{1,0:T(8,128)}) custom-call(s32[1]{0:T(128)} %bitcast.core_ref, bf16[2,2,8,4,16,256]{5,4,3,2,1,0:T(8,128)(2,1)S(1)} %bitcast.12, bf16[2,2,8,4,16,256]{5,4,3,2,1,0:T(8,128)(2,1)S(1)} %collective-permute-done.other_ref, ...), custom_call_target="tpu_custom_call" | custom-call | bytes 4194304 | tf_op jit(solution)/shard_map/pallas_call | solution.py:200
  73.4 0.7 collective-permute-done.1.other_ref
  74.1 1.4 %shard_map.96 = bf16[2,2,2,4,2,4,2,16,256]{8,7,6,5,4,3,2,1,0:T(8,128)(2,1)} custom-call(s32[1]{0:T(128)} %bitcast.core_ref, bf16[2,2,8,4,16,256]{5,4,3,2,1,0:T(8,128)(2,1)S(1)} %bitcast.14, bf16[2,2,8,4,16,256]{5,4,3,2,1,0:T(8,128)(2,1)S(1)} %collective-permute-done.1.other_ref, ...), custom_call_target="tpu_custom_call", output_to_operand_aliasing={{}: (3, {})} | custom-call | bytes 4194304 | tf_op jit(solution)/shard_map/pallas_call | solution.py:207
  (2 shorter events, 0.0 us)
Async XLA Ops:
  67.5 4.6 %collective-permute-start = (bf16[2,2,8,4,16,256]{5,4,3,2,1,0:T(8,128)(2,1)S(1)}, bf16[2,2,8,4,16,256]{5,4,3,2,1,0:T(8,128)(2,1)S(1)}, u32[]{:S(2)}, u32[]{:S(2)}) collective-permute-start(bf16[2,2,8,4,16,256]{5,4,3,2,1,0:T(8,128)(2,1)S(1)} %bitcast.11), channel_id=1, source_target_pairs={{0,64},{64,0},{1,65},{65,1},{2,66},{66,2},{3,67},{67,3},{4,68},{68... | collective-permute-start | bytes 3145736 | tf_op jit(solution)/shard_map/ppermute | solution.py:243
  69.4 4.7 %collective-permute-start.1 = (bf16[2,2,8,4,16,256]{5,4,3,2,1,0:T(8,128)(2,1)S(1)}, bf16[2,2,8,4,16,256]{5,4,3,2,1,0:T(8,128)(2,1)S(1)}, u32[]{:S(2)}, u32[]{:S(2)}) collective-permute-start(bf16[2,2,8,4,16,256]{5,4,3,2,1,0:T(8,128)(2,1)S(1)} %bitcast.13), channel_id=1, source_target_pairs={{0,64},{64,0},{1,65},{65,1},{2,66},{66,2},{3,67},{67,3},{4,68},{68... | collective-permute-start | bytes 3145736 | tf_op jit(solution)/shard_map/ppermute | solution.py:243

commit v7 on v6

--- a/solution.py
+++ b/solution.py
@@ -37,10 +37,10 @@
         return row % 2, row // 2, (y + z) % 2
 
     groups = []
-    for core in BITS:
-        for x in range(core, 4, 2):
-            for y in range(core, 8, 2):
-                for z in range(core, 8, 2):
+    for core, start in enumerate(((0, 0, 1), (1, 1, 0))):
+        for x in range(start[0], 4, 2):
+            for y in range(start[1], 8, 2):
+                for z in range(start[2], 8, 2):
                     cube = [
                         ((x + i) % 4, (y + j) % 8, (z + k) % 8)
                         for i in BITS

time: 75.8 us -> 74.8 us (0.987)
  blocking collectives: 64.8 us -> 63.7 us
    all_to_all x2, blocking collectives: 50.5 us -> 49.3 us  [gather(): lax.all_to_all(copies.reshape((-1,) + value.shape[1:]), AXES, split_axis=...]
where the time goes in v7:
time: 74.8 us; the launch traced here: 74.5 us
  blocking collectives  63.7 us (85%)
  starting transfers between devices  4.33 us (6%)
  Pallas kernels  4.2 us (6%)
  waiting for transfers between devices  1.11 us (1%)
    all_to_all x2, blocking collectives, gather(): lax.all_to_all(copies.reshape((-1,) + value.shape[1:]), AXES, split_axis=...  49.3 us
    all_to_all x1, blocking collectives, per_device(): lax.all_to_all(terms, ('zl', 'c'), split_axis=0, concat_axis=0, tiled=True)  14.3 us
    ppermute x2, starting transfers between devices, per_device(): others = [lax.ppermute(half, 'c', [(0, 1), (1, 0)]) for half in halves]  4.33 us
  transfers between devices with their start and end apart: 2, of which 2 were waited for; matrix products, arithmetic and copies ran while one was open for 0% of the time, Pallas kernels for 2%

profile of v7, /device:TPU:1, one launch (start us, length us, event | category | flops | bytes accessed | tf_op | source)
XLA Modules:
  0.0 74.5 jit_solution(1181107835196703385)
XLA Ops:
  0.6 1.4 %shard_map.94 = (bf16[128,256]{1,0:T(8,128)(2,1)S(1)}, f32[256,256]{1,0:T(8,128)S(1)}, f32[16,256]{1,0:T(8,128)S(1)}, f32[16,256]{1,0:T(8,128)S(1)}, f32[16,256]{1,0:T(8,128)S(1)}, /*index=5*/f32[16,256]{1,0:T(8,128)S(1)}) custom-call(s32[1]{0:T(128)} %bitcast.1.me_ref, f32[128,256]{1,0:T(8,128)} %bitcast.18, s32[1,128]{1,0:T(1,128)} %expo_in.1, ...), custom_call_target="tpu_custom_call" | custom-call | tf_op jit(solution)/shard_map/pallas_call | solution.py:126
  2.1 14.3 %all_to_all.21 = bf16[8,16,256]{2,1,0:T(8,128)(2,1)S(1)} all-to-all(bf16[8,16,256]{2,1,0:T(8,128)(2,1)S(1)} %bitcast.15), channel_id=1, replica_groups=mesh['zl'=4,'c'=2,'x'=4,'zh'=2,'y'=8] {'zl','c'}, dimensions={0} | all-to-all | bytes 131072 | tf_op jit(solution)/shard_map/all_to_all | solution.py:233
  16.4 0.2 clamp_convert_fusion
  16.7 25.8 %all_to_all.22 = bf16[32,16,256]{2,1,0:T(8,128)(2,1)S(1)} all-to-all(bf16[32,16,256]{2,1,0:T(8,128)(2,1)S(1)} %broadcast_in_dim.26), channel_id=1, replica_groups={{0,2,4,6,161,163,165,167,256,258,260,262,417,419,421,423,8,10,12,14,169..., dimensions={0} | all-to-all | bytes 524288 | tf_op jit(solution)/shard_map/all_to_all | solution.py:219
  42.5 0.1 broadcast_in_dim.28
  42.6 23.5 %all_to_all.23 = bf16[8,512,256]{2,1,0:T(8,128)(2,1)S(1)} all-to-all(bf16[8,512,256]{2,1,0:T(8,128)(2,1)S(1)} %broadcast_in_dim.28), channel_id=1, replica_groups={{256,257,129,128,272,273,145,144},{8,9,385,384,24,25,401,400},{264,265,..., dimensions={0} | all-to-all | bytes 4194304 | tf_op jit(solution)/shard_map/all_to_all | solution.py:219
  66.2 0.1 fusion
  66.3 2.3 %collective-permute-start = (bf16[2,2,8,4,16,256]{5,4,3,2,1,0:T(8,128)(2,1)S(1)}, bf16[2,2,8,4,16,256]{5,4,3,2,1,0:T(8,128)(2,1)S(1)}, u32[]{:S(2)}, u32[]{:S(2)}) collective-permute-start(bf16[2,2,8,4,16,256]{5,4,3,2,1,0:T(8,128)(2,1)S(1)} %bitcast.11), channel_id=1, source_target_pairs={{0,64},{64,0},{1,65},{65,1},{2,66},{66,2},{3,67},{67,3},{4,68},{68... | collective-permute-start | bytes 3145736 | tf_op jit(solution)/shard_map/ppermute | solution.py:243
  68.6 2.0 %collective-permute-start.1 = (bf16[2,2,8,4,16,256]{5,4,3,2,1,0:T(8,128)(2,1)S(1)}, bf16[2,2,8,4,16,256]{5,4,3,2,1,0:T(8,128)(2,1)S(1)}, u32[]{:S(2)}, u32[]{:S(2)}) collective-permute-start(bf16[2,2,8,4,16,256]{5,4,3,2,1,0:T(8,128)(2,1)S(1)} %bitcast.13), channel_id=1, source_target_pairs={{0,64},{64,0},{1,65},{65,1},{2,66},{66,2},{3,67},{67,3},{4,68},{68... | collective-permute-start | bytes 3145736 | tf_op jit(solution)/shard_map/ppermute | solution.py:243
  70.6 0.2 collective-permute-done.other_ref
  70.9 1.4 %shard_map.95 = (bf16[2,2,2,4,2,4,2,16,256]{8,7,6,5,4,3,2,1,0:T(8,128)(2,1)}, f32[16,256]{1,0:T(8,128)}, f32[16,256]{1,0:T(8,128)}) custom-call(s32[1]{0:T(128)} %bitcast.core_ref, bf16[2,2,8,4,16,256]{5,4,3,2,1,0:T(8,128)(2,1)S(1)} %bitcast.12, bf16[2,2,8,4,16,256]{5,4,3,2,1,0:T(8,128)(2,1)S(1)} %collective-permute-done.other_ref, ...), custom_call_target="tpu_custom_call" | custom-call | bytes 4194304 | tf_op jit(solution)/shard_map/pallas_call | solution.py:200
  72.3 0.9 %collective-permute-done.1.other_ref = bf16[2,2,8,4,16,256]{5,4,3,2,1,0:T(8,128)(2,1)S(1)} collective-permute-done((bf16[2,2,8,4,16,256]{5,4,3,2,1,0:T(8,128)(2,1)S(1)}, bf16[2,2,8,4,16,256]{5,4,3,2,1,0:T(8,128)(2,1)S(1)}, u32[]{:S(2)}, u32[]{:S(2)}) %collective-permute-start.1) | collective-permute-done | bytes 1048608 | tf_op jit(solution)/shard_map/ppermute | solution.py:243
  73.2 1.4 %shard_map.96 = bf16[2,2,2,4,2,4,2,16,256]{8,7,6,5,4,3,2,1,0:T(8,128)(2,1)} custom-call(s32[1]{0:T(128)} %bitcast.core_ref, bf16[2,2,8,4,16,256]{5,4,3,2,1,0:T(8,128)(2,1)S(1)} %bitcast.14, bf16[2,2,8,4,16,256]{5,4,3,2,1,0:T(8,128)(2,1)S(1)} %collective-permute-done.1.other_ref, ...), custom_call_target="tpu_custom_call", output_to_operand_aliasing={{}: (3, {})} | custom-call | bytes 4194304 | tf_op jit(solution)/shard_map/pallas_call | solution.py:207
  (2 shorter events, 0.0 us)
Async XLA Ops:
  66.3 4.6 %collective-permute-start = (bf16[2,2,8,4,16,256]{5,4,3,2,1,0:T(8,128)(2,1)S(1)}, bf16[2,2,8,4,16,256]{5,4,3,2,1,0:T(8,128)(2,1)S(1)}, u32[]{:S(2)}, u32[]{:S(2)}) collective-permute-start(bf16[2,2,8,4,16,256]{5,4,3,2,1,0:T(8,128)(2,1)S(1)} %bitcast.11), channel_id=1, source_target_pairs={{0,64},{64,0},{1,65},{65,1},{2,66},{66,2},{3,67},{67,3},{4,68},{68... | collective-permute-start | bytes 3145736 | tf_op jit(solution)/shard_map/ppermute | solution.py:243
  68.6 4.6 %collective-permute-start.1 = (bf16[2,2,8,4,16,256]{5,4,3,2,1,0:T(8,128)(2,1)S(1)}, bf16[2,2,8,4,16,256]{5,4,3,2,1,0:T(8,128)(2,1)S(1)}, u32[]{:S(2)}, u32[]{:S(2)}) collective-permute-start(bf16[2,2,8,4,16,256]{5,4,3,2,1,0:T(8,128)(2,1)S(1)} %bitcast.13), channel_id=1, source_target_pairs={{0,64},{64,0},{1,65},{65,1},{2,66},{66,2},{3,67},{67,3},{4,68},{68... | collective-permute-start | bytes 3145736 | tf_op jit(solution)/shard_map/ppermute | solution.py:243

commit v8 on v7

--- a/solution.py
+++ b/solution.py
@@ -10,6 +10,7 @@
 SIZES = (("zl", 4), ("c", 2), ("x", 4), ("zh", 2), ("y", 8))
 AXES = tuple(name for name, _ in SIZES)
 BITS = (0, 1)
+EARLY = 5
 
 
 def device(x, y, z, core):
@@ -153,33 +154,46 @@
     )
 
 
-def fill(core_ref, mine_ref, other_ref, out_ref):
-    xh = pl.program_id(0)
+def fill(core_ref, mine, other, out_ref):
     core = core_ref[0]
-    for side, part_ref in ((core, mine_ref), (1 - core, other_ref)):
-        for zl in range(4):
-            half = xh if zl % 2 == 0 else 1 - xh
-            for py in BITS:
-                for zh in BITS:
-                    out_ref[0, 0, zh, :, py, zl, side] = part_ref[
-                        half, (py + zl) % 2, 4 * zh + zl
-                    ]
+    for xh in BITS:
+
+        @pl.when(pl.program_id(0) == xh)
+        def _():
+            for side, part in ((core, mine), (1 - core, other)):
+                for zl in range(4):
+                    for py in BITS:
+                        for zh in BITS:
+                            out_ref[0, 0, zh, :, py, zl, side] = part(
+                                (xh + zl) % 2, (py + zl) % 2
+                            )[4 * zh + zl]
 
 
 def place_even_kernel(core_ref, mine_ref, other_ref, params_ref, decayed_ref, delta_ref,
                       out_ref, new_params_ref, new_momentum_ref):
-    fill(core_ref, mine_ref, other_ref, out_ref)
+    fill(
+        core_ref,
+        lambda half, side: mine_ref.at[2 * half + side],
+        lambda half, side: other_ref.at[2 * half + side],
+        out_ref,
+    )
     delta = delta_ref[...]
     new_momentum = decayed_ref[...] + delta
     new_momentum_ref[...] = new_momentum
     new_params_ref[...] = params_ref[...] - 0.7 * (delta + 0.9 * new_momentum)
 
 
-def place_odd_kernel(core_ref, mine_ref, other_ref, even_ref, out_ref):
-    fill(core_ref, mine_ref, other_ref, out_ref)
-
-
-def place(core, mine, other, owner=None, even=None):
+def place_odd_kernel(core_ref, mine_ref, early_ref, late_ref, even_ref, out_ref):
+    early = early_ref.shape[0]
+
+    def other(half, side):
+        at = 4 + 2 * half + side
+        return early_ref.at[at] if at < early else late_ref.at[at - early]
+
+    fill(core_ref, lambda half, side: mine_ref.at[4 + 2 * half + side], other, out_ref)
+
+
+def place(core, mine, early, owner=None, late=None, even=None):
     owned, width = mine.shape[-2:]
     px = 0 if even is None else 1
     block = (2, 4, 2, 4, 2, owned, width)
@@ -192,7 +206,7 @@
     common = dict(
         grid=(2,),
         cost_estimate=pl.CostEstimate(
-            flops=0, bytes_accessed=8 * mine.size, transcendentals=0
+            flops=0, bytes_accessed=4 * mine.size, transcendentals=0
         ),
         compiler_params=pltpu.CompilerParams(vmem_limit_bytes=16 * 2**20),
     )
@@ -203,15 +217,15 @@
             in_specs=[smem] + [vmem] * 5,
             out_specs=(whole_spec, small_spec, small_spec),
             **common,
-        )(core, mine, other, *owner)
+        )(core, mine, early, *owner)
     return pl.pallas_call(
         place_odd_kernel,
         out_shape=whole,
-        in_specs=[smem, vmem, vmem, pl.BlockSpec(memory_space=pl.ANY)],
+        in_specs=[smem, vmem, vmem, vmem, pl.BlockSpec(memory_space=pl.ANY)],
         out_specs=whole_spec,
-        input_output_aliases={3: 0},
+        input_output_aliases={4: 0},
         **common,
-    )(core, mine, other, even)
+    )(core, mine, early, late, even)
 
 
 def gather(value, groups):
@@ -237,15 +251,15 @@
     new_params = params - 0.7 * (delta + 0.9 * (decayed + delta))
     codes = jnp.clip(new_params * inverse, -4.0, 4.0).astype(jnp.bfloat16)
     mine = gather(gather(codes, classes()), cubes())
-    halves = [
-        half.reshape(2, 2, 8, 4, owned, width) for half in jnp.split(mine, 2)
-    ]
-    others = [lax.ppermute(half, "c", [(0, 1), (1, 0)]) for half in halves]
+    mine = mine.reshape(8, 8, 4, owned, width)
+    early, late = (
+        lax.ppermute(part, "c", [(0, 1), (1, 0)]) for part in (mine[:EARLY], mine[EARLY:])
+    )
     core = lax.axis_index("c").astype(jnp.int32)[None]
     whole, new_params, new_momentum = place(
-        core, halves[0], others[0], owner=(params, decayed, delta)
-    )
-    whole = place(core, halves[1], others[1], even=whole)
+        core, mine, early, owner=(params, decayed, delta)
+    )
+    whole = place(core, mine, early, late=late, even=whole)
     return new_params, new_momentum, whole.reshape(-1, width)
 
 

time: 74.8 us -> 74.5 us (level)
  no operation moved by 1% of the time
where the time goes in v8:
time: 74.5 us; the launch traced here: 74.2 us
  blocking collectives  63.7 us (86%)
  starting transfers between devices  4.33 us (6%)
  Pallas kernels  4.2 us (6%)
    all_to_all x2, blocking collectives, gather(): lax.all_to_all(copies.reshape((-1,) + value.shape[1:]), AXES, split_axis=...  49.3 us
    all_to_all x1, blocking collectives, per_device(): lax.all_to_all(terms, ('zl', 'c'), split_axis=0, concat_axis=0, tiled=True)  14.3 us
    ppermute x2, starting transfers between devices, per_device(): lax.ppermute(part, 'c', [(0, 1), (1, 0)])  4.33 us
  transfers between devices with their start and end apart: 2, of which 2 were waited for; matrix products, arithmetic and copies ran while one was open for 0% of the time, Pallas kernels for 2%

profile of v8, /device:TPU:1, one launch (start us, length us, event | category | flops | bytes accessed | tf_op | source)
XLA Modules:
  0.0 74.2 jit_solution(13967998584812826325)
XLA Ops:
  0.6 1.4 %shard_map.94 = (bf16[128,256]{1,0:T(8,128)(2,1)S(1)}, f32[256,256]{1,0:T(8,128)S(1)}, f32[16,256]{1,0:T(8,128)S(1)}, f32[16,256]{1,0:T(8,128)S(1)}, f32[16,256]{1,0:T(8,128)S(1)}, /*index=5*/f32[16,256]{1,0:T(8,128)S(1)}) custom-call(s32[1]{0:T(128)} %bitcast.1.me_ref, f32[128,256]{1,0:T(8,128)} %bitcast.19, s32[1,128]{1,0:T(1,128)} %expo_in.1, ...), custom_call_target="tpu_custom_call" | custom-call | tf_op jit(solution)/shard_map/pallas_call | solution.py:127
  2.1 14.3 %all_to_all.21 = bf16[8,16,256]{2,1,0:T(8,128)(2,1)S(1)} all-to-all(bf16[8,16,256]{2,1,0:T(8,128)(2,1)S(1)} %bitcast.14), channel_id=1, replica_groups=mesh['zl'=4,'c'=2,'x'=4,'zh'=2,'y'=8] {'zl','c'}, dimensions={0} | all-to-all | bytes 131072 | tf_op jit(solution)/shard_map/all_to_all | solution.py:247
  16.4 0.2 clamp_convert_fusion
  16.7 25.8 %all_to_all.22 = bf16[32,16,256]{2,1,0:T(8,128)(2,1)S(1)} all-to-all(bf16[32,16,256]{2,1,0:T(8,128)(2,1)S(1)} %broadcast_in_dim.26), channel_id=1, replica_groups={{0,2,4,6,161,163,165,167,256,258,260,262,417,419,421,423,8,10,12,14,169..., dimensions={0} | all-to-all | bytes 524288 | tf_op jit(solution)/shard_map/all_to_all | solution.py:233
  42.5 0.1 broadcast_in_dim.28
  42.6 23.5 %all_to_all.23 = bf16[8,512,256]{2,1,0:T(8,128)(2,1)S(1)} all-to-all(bf16[8,512,256]{2,1,0:T(8,128)(2,1)S(1)} %broadcast_in_dim.28), channel_id=1, replica_groups={{256,257,129,128,272,273,145,144},{8,9,385,384,24,25,401,400},{264,265,..., dimensions={0} | all-to-all | bytes 4194304 | tf_op jit(solution)/shard_map/all_to_all | solution.py:233
  66.2 0.1 slice.18
  66.2 2.3 %collective-permute-start = (bf16[5,8,4,16,256]{4,3,2,1,0:T(8,128)(2,1)S(1)}, bf16[5,8,4,16,256]{4,3,2,1,0:T(8,128)(2,1)S(1)}, u32[]{:S(2)}, u32[]{:S(2)}) collective-permute-start(bf16[5,8,4,16,256]{4,3,2,1,0:T(8,128)(2,1)S(1)} %bitcast.16), channel_id=1, source_target_pairs={{0,64},{64,0},{1,65},{65,1},{2,66},{66,2},{3,67},{67,3},{4,68},{68... | collective-permute-start | bytes 3932168 | tf_op jit(solution)/shard_map/ppermute | solution.py:256
  68.5 0.1 slice.19
  68.6 2.0 %collective-permute-start.1 = (bf16[3,8,4,16,256]{4,3,2,1,0:T(8,128)(2,1)S(1)}, bf16[3,8,4,16,256]{4,3,2,1,0:T(8,128)(2,1)S(1)}, u32[]{:S(2)}, u32[]{:S(2)}) collective-permute-start(bf16[3,8,4,16,256]{4,3,2,1,0:T(8,128)(2,1)S(1)} %bitcast.18), channel_id=1, source_target_pairs={{0,64},{64,0},{1,65},{65,1},{2,66},{66,2},{3,67},{67,3},{4,68},{68... | collective-permute-start | bytes 2359304 | tf_op jit(solution)/shard_map/ppermute | solution.py:256
  70.6 0.5 collective-permute-done.other_ref.early_ref
  71.2 1.4 %shard_map.95 = (bf16[2,2,2,4,2,4,2,16,256]{8,7,6,5,4,3,2,1,0:T(8,128)(2,1)}, f32[16,256]{1,0:T(8,128)}, f32[16,256]{1,0:T(8,128)}) custom-call(s32[1]{0:T(128)} %bitcast.core_ref, bf16[8,8,4,16,256]{4,3,2,1,0:T(8,128)(2,1)S(1)} %bitcast.12, bf16[5,8,4,16,256]{4,3,2,1,0:T(8,128)(2,1)S(1)} %collective-permute-done.other_ref.early_ref, ...), custom_call_target="tpu_custom_call" | custom-call | bytes 4194304 | tf_op jit(solution)/shard_map/pallas_call | solution.py:214
  72.6 0.2 collective-permute-done.1.late_ref
  72.8 1.4 %shard_map.96 = bf16[2,2,2,4,2,4,2,16,256]{8,7,6,5,4,3,2,1,0:T(8,128)(2,1)} custom-call(s32[1]{0:T(128)} %bitcast.core_ref, bf16[8,8,4,16,256]{4,3,2,1,0:T(8,128)(2,1)S(1)} %bitcast.13, bf16[5,8,4,16,256]{4,3,2,1,0:T(8,128)(2,1)S(1)} %collective-permute-done.other_ref.early_ref, ...), custom_call_target="tpu_custom_call", output_to_operand_aliasing={{}: (4, {})} | custom-call | bytes 4194304 | tf_op jit(solution)/shard_map/pallas_call | solution.py:221
  (2 shorter events, 0.0 us)
Async XLA Ops:
  66.2 4.9 %collective-permute-start = (bf16[5,8,4,16,256]{4,3,2,1,0:T(8,128)(2,1)S(1)}, bf16[5,8,4,16,256]{4,3,2,1,0:T(8,128)(2,1)S(1)}, u32[]{:S(2)}, u32[]{:S(2)}) collective-permute-start(bf16[5,8,4,16,256]{4,3,2,1,0:T(8,128)(2,1)S(1)} %bitcast.16), channel_id=1, source_target_pairs={{0,64},{64,0},{1,65},{65,1},{2,66},{66,2},{3,67},{67,3},{4,68},{68... | collective-permute-start | bytes 3932168 | tf_op jit(solution)/shard_map/ppermute | solution.py:256
  68.6 4.2 %collective-permute-start.1 = (bf16[3,8,4,16,256]{4,3,2,1,0:T(8,128)(2,1)S(1)}, bf16[3,8,4,16,256]{4,3,2,1,0:T(8,128)(2,1)S(1)}, u32[]{:S(2)}, u32[]{:S(2)}) collective-permute-start(bf16[3,8,4,16,256]{4,3,2,1,0:T(8,128)(2,1)S(1)} %bitcast.18), channel_id=1, source_target_pairs={{0,64},{64,0},{1,65},{65,1},{2,66},{66,2},{3,67},{67,3},{4,68},{68... | collective-permute-start | bytes 2359304 | tf_op jit(solution)/shard_map/ppermute | solution.py:256

commit v9 on v8

--- a/solution.py
+++ b/solution.py
@@ -62,14 +62,12 @@
     return (1 - 2 * (parity % 2)).astype(np.float32)
 
 
-def exact_dot(values, table):
-    total = None
-    for _ in range(3):
-        part = values.astype(jnp.bfloat16)
-        values = values - part.astype(jnp.float32)
-        product = jnp.dot(part, table, preferred_element_type=jnp.float32)
-        total = product if total is None else total + product
-    return total
+def dot_parts(values, table):
+    high = values.astype(jnp.bfloat16)
+    low = (values - high.astype(jnp.float32)).astype(jnp.bfloat16)
+    parts = jnp.concatenate([high, low])
+    both = jnp.dot(parts, table, preferred_element_type=jnp.float32)
+    return both[: values.shape[0]] + both[values.shape[0] :]
 
 
 def column(row):
@@ -105,8 +103,7 @@
     owned = own_sign_ref.shape[0]
     replicas = grad_ref.shape[0] // owned
     sign = (2 * bits_ref[...] - 1).astype(jnp.float32)
-    table = table_ref[...].astype(jnp.bfloat16)
-    rotated = exact_dot(grad_ref[...] * sign, table) * (width**-0.5)
+    rotated = dot_parts(grad_ref[...] * sign, table_ref[...]) * (width**-0.5)
     limit = column(4.0 * jnp.exp2(expo_ref[...].astype(jnp.float32)))
     terms_ref[...] = jnp.clip(rotated, -limit, limit).astype(terms_ref.dtype)
     own = pl.ds(pl.multiple_of(me_ref[0] * owned, owned), owned)
@@ -128,7 +125,7 @@
         encode_kernel,
         out_shape=(
             jax.ShapeDtypeStruct((shard, width), jnp.bfloat16),
-            jax.ShapeDtypeStruct((width, width), f32),
+            jax.ShapeDtypeStruct((width, width), jnp.bfloat16),
             jax.ShapeDtypeStruct((owned, width), f32),
             jax.ShapeDtypeStruct((owned, width), f32),
             jax.ShapeDtypeStruct((owned, width), f32),
@@ -240,14 +237,19 @@
     owned, width = params.shape
     replicas = lax.axis_size(("zl", "c"))
     me = lax.axis_index(("zl", "c")).astype(jnp.int32)[None]
-    table = jnp.asarray(hadamard(width))
+    table = jnp.asarray(hadamard(width), jnp.bfloat16)
     terms, table, params, decayed, own_sign, inverse = encode(
         me, pseudo_grad[0], grad_expo, sign_bits, table, params, momentum, param_expo[None]
     )
     terms = lax.all_to_all(terms, ("zl", "c"), split_axis=0, concat_axis=0, tiled=True)
 
     total = jnp.sum(terms.reshape(replicas, owned, width).astype(jnp.float32), axis=0)
-    delta = jnp.dot(total, table, precision=lax.Precision.HIGHEST) * own_sign
+    high = lax.reduce_precision(total, 8, 7)
+    delta = sum(
+        jnp.dot(part.astype(jnp.bfloat16), table, preferred_element_type=jnp.float32)
+        for part in (high, total - high)
+    )
+    delta = delta * own_sign
     new_params = params - 0.7 * (delta + 0.9 * (decayed + delta))
     codes = jnp.clip(new_params * inverse, -4.0, 4.0).astype(jnp.bfloat16)
     mine = gather(gather(codes, classes()), cubes())

time: 74.5 us -> 74.4 us (level)
  no operation moved by 1% of the time
where the time goes in v9:
time: 74.4 us; the launch traced here: 74.2 us
  blocking collectives  63.7 us (86%)
  starting transfers between devices  4.33 us (6%)
  Pallas kernels  4.11 us (6%)
    all_to_all x2, blocking collectives, gather(): lax.all_to_all(copies.reshape((-1,) + value.shape[1:]), AXES, split_axis=...  49.3 us
    all_to_all x1, blocking collectives, per_device(): lax.all_to_all(terms, ('zl', 'c'), split_axis=0, concat_axis=0, tiled=True)  14.3 us
    ppermute x2, starting transfers between devices, per_device(): lax.ppermute(part, 'c', [(0, 1), (1, 0)])  4.33 us
  transfers between devices with their start and end apart: 2, of which 2 were waited for; matrix products, arithmetic and copies ran while one was open for 0% of the time, Pallas kernels for 2%

profile of v9, /device:TPU:1, one launch (start us, length us, event | category | flops | bytes accessed | tf_op | source)
XLA Modules:
  0.0 74.2 jit_solution(17113507901054826016)
XLA Ops:
  0.6 1.3 %shard_map.94 = (bf16[128,256]{1,0:T(8,128)(2,1)S(1)}, bf16[256,256]{1,0:T(8,128)(2,1)S(1)}, f32[16,256]{1,0:T(8,128)S(1)}, f32[16,256]{1,0:T(8,128)S(1)}, f32[16,256]{1,0:T(8,128)S(1)}, /*index=5*/f32[16,256]{1,0:T(8,128)S(1)}) custom-call(s32[1]{0:T(128)} %bitcast.1.me_ref, f32[128,256]{1,0:T(8,128)} %bitcast.19, s32[1,128]{1,0:T(1,128)} %expo_in.1, ...), custom_call_target="tpu_custom_call" | custom-call | tf_op jit(solution)/shard_map/pallas_call | solution.py:124
  2.0 14.3 %all_to_all.21 = bf16[8,16,256]{2,1,0:T(8,128)(2,1)S(1)} all-to-all(bf16[8,16,256]{2,1,0:T(8,128)(2,1)S(1)} %bitcast.14), channel_id=1, replica_groups=mesh['zl'=4,'c'=2,'x'=4,'zh'=2,'y'=8] {'zl','c'}, dimensions={0} | all-to-all | bytes 131072 | tf_op jit(solution)/shard_map/all_to_all | solution.py:244
  16.3 0.1 fusion.3
  16.4 0.2 clamp_convert_fusion
  16.7 25.8 %all_to_all.22 = bf16[32,16,256]{2,1,0:T(8,128)(2,1)S(1)} all-to-all(bf16[32,16,256]{2,1,0:T(8,128)(2,1)S(1)} %broadcast_in_dim.26), channel_id=1, replica_groups={{0,2,4,6,161,163,165,167,256,258,260,262,417,419,421,423,8,10,12,14,169..., dimensions={0} | all-to-all | bytes 524288 | tf_op jit(solution)/shard_map/all_to_all | solution.py:230
  42.4 0.1 broadcast_in_dim.28
  42.6 23.5 %all_to_all.23 = bf16[8,512,256]{2,1,0:T(8,128)(2,1)S(1)} all-to-all(bf16[8,512,256]{2,1,0:T(8,128)(2,1)S(1)} %broadcast_in_dim.28), channel_id=1, replica_groups={{256,257,129,128,272,273,145,144},{8,9,385,384,24,25,401,400},{264,265,..., dimensions={0} | all-to-all | bytes 4194304 | tf_op jit(solution)/shard_map/all_to_all | solution.py:230
  66.1 0.1 slice.18
  66.2 2.3 %collective-permute-start = (bf16[5,8,4,16,256]{4,3,2,1,0:T(8,128)(2,1)S(1)}, bf16[5,8,4,16,256]{4,3,2,1,0:T(8,128)(2,1)S(1)}, u32[]{:S(2)}, u32[]{:S(2)}) collective-permute-start(bf16[5,8,4,16,256]{4,3,2,1,0:T(8,128)(2,1)S(1)} %bitcast.16), channel_id=1, source_target_pairs={{0,64},{64,0},{1,65},{65,1},{2,66},{66,2},{3,67},{67,3},{4,68},{68... | collective-permute-start | bytes 3932168 | tf_op jit(solution)/shard_map/ppermute | solution.py:258
  68.5 0.1 slice.19
  68.6 2.0 %collective-permute-start.1 = (bf16[3,8,4,16,256]{4,3,2,1,0:T(8,128)(2,1)S(1)}, bf16[3,8,4,16,256]{4,3,2,1,0:T(8,128)(2,1)S(1)}, u32[]{:S(2)}, u32[]{:S(2)}) collective-permute-start(bf16[3,8,4,16,256]{4,3,2,1,0:T(8,128)(2,1)S(1)} %bitcast.18), channel_id=1, source_target_pairs={{0,64},{64,0},{1,65},{65,1},{2,66},{66,2},{3,67},{67,3},{4,68},{68... | collective-permute-start | bytes 2359304 | tf_op jit(solution)/shard_map/ppermute | solution.py:258
  70.6 0.5 collective-permute-done.other_ref.early_ref
  71.2 1.4 %shard_map.95 = (bf16[2,2,2,4,2,4,2,16,256]{8,7,6,5,4,3,2,1,0:T(8,128)(2,1)}, f32[16,256]{1,0:T(8,128)}, f32[16,256]{1,0:T(8,128)}) custom-call(s32[1]{0:T(128)} %bitcast.core_ref, bf16[8,8,4,16,256]{4,3,2,1,0:T(8,128)(2,1)S(1)} %bitcast.12, bf16[5,8,4,16,256]{4,3,2,1,0:T(8,128)(2,1)S(1)} %collective-permute-done.other_ref.early_ref, ...), custom_call_target="tpu_custom_call" | custom-call | bytes 4194304 | tf_op jit(solution)/shard_map/pallas_call | solution.py:211
  72.6 0.2 collective-permute-done.1.late_ref
  72.8 1.4 %shard_map.96 = bf16[2,2,2,4,2,4,2,16,256]{8,7,6,5,4,3,2,1,0:T(8,128)(2,1)} custom-call(s32[1]{0:T(128)} %bitcast.core_ref, bf16[8,8,4,16,256]{4,3,2,1,0:T(8,128)(2,1)S(1)} %bitcast.13, bf16[5,8,4,16,256]{4,3,2,1,0:T(8,128)(2,1)S(1)} %collective-permute-done.other_ref.early_ref, ...), custom_call_target="tpu_custom_call", output_to_operand_aliasing={{}: (4, {})} | custom-call | bytes 4194304 | tf_op jit(solution)/shard_map/pallas_call | solution.py:218
  (2 shorter events, 0.0 us)
Async XLA Ops:
  66.2 4.9 %collective-permute-start = (bf16[5,8,4,16,256]{4,3,2,1,0:T(8,128)(2,1)S(1)}, bf16[5,8,4,16,256]{4,3,2,1,0:T(8,128)(2,1)S(1)}, u32[]{:S(2)}, u32[]{:S(2)}) collective-permute-start(bf16[5,8,4,16,256]{4,3,2,1,0:T(8,128)(2,1)S(1)} %bitcast.16), channel_id=1, source_target_pairs={{0,64},{64,0},{1,65},{65,1},{2,66},{66,2},{3,67},{67,3},{4,68},{68... | collective-permute-start | bytes 3932168 | tf_op jit(solution)/shard_map/ppermute | solution.py:258
  68.6 4.2 %collective-permute-start.1 = (bf16[3,8,4,16,256]{4,3,2,1,0:T(8,128)(2,1)S(1)}, bf16[3,8,4,16,256]{4,3,2,1,0:T(8,128)(2,1)S(1)}, u32[]{:S(2)}, u32[]{:S(2)}) collective-permute-start(bf16[3,8,4,16,256]{4,3,2,1,0:T(8,128)(2,1)S(1)} %bitcast.18), channel_id=1, source_target_pairs={{0,64},{64,0},{1,65},{65,1},{2,66},{66,2},{3,67},{67,3},{4,68},{68... | collective-permute-start | bytes 2359304 | tf_op jit(solution)/shard_map/ppermute | solution.py:258

commit v10 on v8

--- a/solution.py
+++ b/solution.py
@@ -156,6 +156,7 @@
 
 def fill(core_ref, mine, other, out_ref):
     core = core_ref[0]
+    zh = pl.program_id(1)
     for xh in BITS:
 
         @pl.when(pl.program_id(0) == xh)
@@ -163,10 +164,9 @@
             for side, part in ((core, mine), (1 - core, other)):
                 for zl in range(4):
                     for py in BITS:
-                        for zh in BITS:
-                            out_ref[0, 0, zh, :, py, zl, side] = part(
-                                (xh + zl) % 2, (py + zl) % 2
-                            )[4 * zh + zl]
+                        out_ref[0, 0, 0, :, py, zl, side] = part(
+                            (xh + zl) % 2, (py + zl) % 2
+                        )[4 * zh + zl]
 
 
 def place_even_kernel(core_ref, mine_ref, other_ref, params_ref, decayed_ref, delta_ref,
@@ -196,15 +196,17 @@
 def place(core, mine, early, owner=None, late=None, even=None):
     owned, width = mine.shape[-2:]
     px = 0 if even is None else 1
-    block = (2, 4, 2, 4, 2, owned, width)
+    block = (4, 2, 4, 2, owned, width)
     smem = pl.BlockSpec(memory_space=pltpu.SMEM)
     vmem = pl.BlockSpec(memory_space=pltpu.VMEM)
-    whole = jax.ShapeDtypeStruct((2, 2) + block, mine.dtype)
-    whole_spec = pl.BlockSpec((1, 1) + block, lambda xh: (xh, px) + (0,) * len(block))
+    whole = jax.ShapeDtypeStruct((2, 2, 2) + block, mine.dtype)
+    whole_spec = pl.BlockSpec(
+        (1, 1, 1) + block, lambda xh, zh: (xh, px, zh) + (0,) * len(block)
+    )
     small = jax.ShapeDtypeStruct((owned, width), jnp.float32)
-    small_spec = pl.BlockSpec((owned, width), lambda xh: (0, 0))
+    small_spec = pl.BlockSpec((owned, width), lambda xh, zh: (0, 0))
     common = dict(
-        grid=(2,),
+        grid=(2, 2),
         cost_estimate=pl.CostEstimate(
             flops=0, bytes_accessed=4 * mine.size, transcendentals=0
         ),

time: 74.5 us -> 75.2 us (level)
  Pallas kernels: 4.2 us -> 5.1 us
  transfers between devices with their start and end apart: 2 -> 2, of which waited for: 2 -> 1; matrix products, arithmetic and copies ran while one was open for 0% -> 0% of each run, Pallas kernels for 2% -> 2%
where the time goes in v10:
time: 75.2 us; the launch traced here: 74.9 us
  blocking collectives  63.7 us (85%)
  Pallas kernels  5.1 us (7%)
  starting transfers between devices  4.33 us (6%)
    all_to_all x2, blocking collectives, gather(): lax.all_to_all(copies.reshape((-1,) + value.shape[1:]), AXES, split_axis=...  49.3 us
    all_to_all x1, blocking collectives, per_device(): lax.all_to_all(terms, ('zl', 'c'), split_axis=0, concat_axis=0, tiled=True)  14.3 us
    ppermute x2, starting transfers between devices, per_device(): lax.ppermute(part, 'c', [(0, 1), (1, 0)])  4.33 us
    pallas_call x1, Pallas kernels, place(): pl.pallas_call(place_odd_kernel, out_shape=whole, in_specs=[smem, vmem, v...  1.86 us
    pallas_call x1, Pallas kernels, place(): pl.pallas_call(place_even_kernel, out_shape=(whole, small, small), in_spe...  1.84 us
  transfers between devices with their start and end apart: 2, of which 1 were waited for; matrix products, arithmetic and copies ran while one was open for 0% of the time, Pallas kernels for 2%

profile of v10, /device:TPU:1, one launch (start us, length us, event | category | flops | bytes accessed | tf_op | source)
XLA Modules:
  0.0 74.9 jit_solution(13133986439103600710)
XLA Ops:
  0.6 1.4 %shard_map.94 = (bf16[128,256]{1,0:T(8,128)(2,1)S(1)}, f32[256,256]{1,0:T(8,128)S(1)}, f32[16,256]{1,0:T(8,128)S(1)}, f32[16,256]{1,0:T(8,128)S(1)}, f32[16,256]{1,0:T(8,128)S(1)}, /*index=5*/f32[16,256]{1,0:T(8,128)S(1)}) custom-call(s32[1]{0:T(128)} %bitcast.1.me_ref, f32[128,256]{1,0:T(8,128)} %bitcast.19, s32[1,128]{1,0:T(1,128)} %expo_in.1, ...), custom_call_target="tpu_custom_call" | custom-call | tf_op jit(solution)/shard_map/pallas_call | solution.py:127
  2.1 14.3 %all_to_all.21 = bf16[8,16,256]{2,1,0:T(8,128)(2,1)S(1)} all-to-all(bf16[8,16,256]{2,1,0:T(8,128)(2,1)S(1)} %bitcast.14), channel_id=1, replica_groups=mesh['zl'=4,'c'=2,'x'=4,'zh'=2,'y'=8] {'zl','c'}, dimensions={0} | all-to-all | bytes 131072 | tf_op jit(solution)/shard_map/all_to_all | solution.py:249
  16.4 0.2 clamp_convert_fusion
  16.7 25.8 %all_to_all.22 = bf16[32,16,256]{2,1,0:T(8,128)(2,1)S(1)} all-to-all(bf16[32,16,256]{2,1,0:T(8,128)(2,1)S(1)} %broadcast_in_dim.26), channel_id=1, replica_groups={{0,2,4,6,161,163,165,167,256,258,260,262,417,419,421,423,8,10,12,14,169..., dimensions={0} | all-to-all | bytes 524288 | tf_op jit(solution)/shard_map/all_to_all | solution.py:235
  42.5 0.1 broadcast_in_dim.28
  42.6 23.5 %all_to_all.23 = bf16[8,512,256]{2,1,0:T(8,128)(2,1)S(1)} all-to-all(bf16[8,512,256]{2,1,0:T(8,128)(2,1)S(1)} %broadcast_in_dim.28), channel_id=1, replica_groups={{256,257,129,128,272,273,145,144},{8,9,385,384,24,25,401,400},{264,265,..., dimensions={0} | all-to-all | bytes 4194304 | tf_op jit(solution)/shard_map/all_to_all | solution.py:235
  66.2 0.1 slice.18
  66.2 2.3 %collective-permute-start = (bf16[5,8,4,16,256]{4,3,2,1,0:T(8,128)(2,1)S(1)}, bf16[5,8,4,16,256]{4,3,2,1,0:T(8,128)(2,1)S(1)}, u32[]{:S(2)}, u32[]{:S(2)}) collective-permute-start(bf16[5,8,4,16,256]{4,3,2,1,0:T(8,128)(2,1)S(1)} %bitcast.16), channel_id=1, source_target_pairs={{0,64},{64,0},{1,65},{65,1},{2,66},{66,2},{3,67},{67,3},{4,68},{68... | collective-permute-start | bytes 3932168 | tf_op jit(solution)/shard_map/ppermute | solution.py:258
  68.5 0.1 slice.19
  68.6 2.0 %collective-permute-start.1 = (bf16[3,8,4,16,256]{4,3,2,1,0:T(8,128)(2,1)S(1)}, bf16[3,8,4,16,256]{4,3,2,1,0:T(8,128)(2,1)S(1)}, u32[]{:S(2)}, u32[]{:S(2)}) collective-permute-start(bf16[3,8,4,16,256]{4,3,2,1,0:T(8,128)(2,1)S(1)} %bitcast.18), channel_id=1, source_target_pairs={{0,64},{64,0},{1,65},{65,1},{2,66},{66,2},{3,67},{67,3},{4,68},{68... | collective-permute-start | bytes 2359304 | tf_op jit(solution)/shard_map/ppermute | solution.py:258
  70.6 0.5 collective-permute-done.other_ref.early_ref
  71.2 1.8 %shard_map.95 = (bf16[2,2,2,4,2,4,2,16,256]{8,7,6,5,4,3,2,1,0:T(8,128)(2,1)}, f32[16,256]{1,0:T(8,128)}, f32[16,256]{1,0:T(8,128)}) custom-call(s32[1]{0:T(128)} %bitcast.core_ref, bf16[8,8,4,16,256]{4,3,2,1,0:T(8,128)(2,1)S(1)} %bitcast.12, bf16[5,8,4,16,256]{4,3,2,1,0:T(8,128)(2,1)S(1)} %collective-permute-done.other_ref.early_ref, ...), custom_call_target="tpu_custom_call" | custom-call | bytes 4194304 | tf_op jit(solution)/shard_map/pallas_call | solution.py:216
  73.0 0.0 collective-permute-done.1.late_ref
  73.0 1.9 %shard_map.96 = bf16[2,2,2,4,2,4,2,16,256]{8,7,6,5,4,3,2,1,0:T(8,128)(2,1)} custom-call(s32[1]{0:T(128)} %bitcast.core_ref, bf16[8,8,4,16,256]{4,3,2,1,0:T(8,128)(2,1)S(1)} %bitcast.13, bf16[5,8,4,16,256]{4,3,2,1,0:T(8,128)(2,1)S(1)} %collective-permute-done.other_ref.early_ref, ...), custom_call_target="tpu_custom_call", output_to_operand_aliasing={{}: (4, {})} | custom-call | bytes 4194304 | tf_op jit(solution)/shard_map/pallas_call | solution.py:223
  (2 shorter events, 0.0 us)
Async XLA Ops:
  66.2 4.9 %collective-permute-start = (bf16[5,8,4,16,256]{4,3,2,1,0:T(8,128)(2,1)S(1)}, bf16[5,8,4,16,256]{4,3,2,1,0:T(8,128)(2,1)S(1)}, u32[]{:S(2)}, u32[]{:S(2)}) collective-permute-start(bf16[5,8,4,16,256]{4,3,2,1,0:T(8,128)(2,1)S(1)} %bitcast.16), channel_id=1, source_target_pairs={{0,64},{64,0},{1,65},{65,1},{2,66},{66,2},{3,67},{67,3},{4,68},{68... | collective-permute-start | bytes 3932168 | tf_op jit(solution)/shard_map/ppermute | solution.py:258
  68.6 4.4 %collective-permute-start.1 = (bf16[3,8,4,16,256]{4,3,2,1,0:T(8,128)(2,1)S(1)}, bf16[3,8,4,16,256]{4,3,2,1,0:T(8,128)(2,1)S(1)}, u32[]{:S(2)}, u32[]{:S(2)}) collective-permute-start(bf16[3,8,4,16,256]{4,3,2,1,0:T(8,128)(2,1)S(1)} %bitcast.18), channel_id=1, source_target_pairs={{0,64},{64,0},{1,65},{65,1},{2,66},{66,2},{3,67},{67,3},{4,68},{68... | collective-permute-start | bytes 2359304 | tf_op jit(solution)/shard_map/ppermute | solution.py:258

commit v11 on v8

--- a/solution.py
+++ b/solution.py
@@ -157,16 +157,13 @@
 def fill(core_ref, mine, other, out_ref):
     core = core_ref[0]
     for xh in BITS:
-
-        @pl.when(pl.program_id(0) == xh)
-        def _():
-            for side, part in ((core, mine), (1 - core, other)):
-                for zl in range(4):
-                    for py in BITS:
-                        for zh in BITS:
-                            out_ref[0, 0, zh, :, py, zl, side] = part(
-                                (xh + zl) % 2, (py + zl) % 2
-                            )[4 * zh + zl]
+        for side, part in ((core, mine), (1 - core, other)):
+            for zl in range(4):
+                for py in BITS:
+                    for zh in BITS:
+                        out_ref[xh, 0, zh, :, py, zl, side] = part(
+                            (xh + zl) % 2, (py + zl) % 2
+                        )[4 * zh + zl]
 
 
 def place_even_kernel(core_ref, mine_ref, other_ref, params_ref, decayed_ref, delta_ref,
@@ -200,11 +197,11 @@
     smem = pl.BlockSpec(memory_space=pltpu.SMEM)
     vmem = pl.BlockSpec(memory_space=pltpu.VMEM)
     whole = jax.ShapeDtypeStruct((2, 2) + block, mine.dtype)
-    whole_spec = pl.BlockSpec((1, 1) + block, lambda xh: (xh, px) + (0,) * len(block))
+    whole_spec = pl.BlockSpec((2, 1) + block, lambda i: (0, px) + (0,) * len(block))
     small = jax.ShapeDtypeStruct((owned, width), jnp.float32)
-    small_spec = pl.BlockSpec((owned, width), lambda xh: (0, 0))
+    small_spec = pl.BlockSpec((owned, width), lambda i: (0, 0))
     common = dict(
-        grid=(2,),
+        grid=(1,),
         cost_estimate=pl.CostEstimate(
             flops=0, bytes_accessed=4 * mine.size, transcendentals=0
         ),

time: 74.5 us -> 74.5 us (level)
  no operation moved by 1% of the time
where the time goes in v11:
time: 74.5 us; the launch traced here: 74.3 us
  blocking collectives  63.7 us (86%)
  Pallas kernels  4.36 us (6%)
  starting transfers between devices  4.33 us (6%)
    all_to_all x2, blocking collectives, gather(): lax.all_to_all(copies.reshape((-1,) + value.shape[1:]), AXES, split_axis=...  49.3 us
    all_to_all x1, blocking collectives, per_device(): lax.all_to_all(terms, ('zl', 'c'), split_axis=0, concat_axis=0, tiled=True)  14.3 us
    ppermute x2, starting transfers between devices, per_device(): lax.ppermute(part, 'c', [(0, 1), (1, 0)])  4.33 us
  transfers between devices with their start and end apart: 2, of which 2 were waited for; matrix products, arithmetic and copies ran while one was open for 0% of the time, Pallas kernels for 2%

profile of v11, /device:TPU:1, one launch (start us, length us, event | category | flops | bytes accessed | tf_op | source)
XLA Modules:
  0.0 74.3 jit_solution(4619218049667644200)
XLA Ops:
  0.6 1.4 %shard_map.94 = (bf16[128,256]{1,0:T(8,128)(2,1)S(1)}, f32[256,256]{1,0:T(8,128)S(1)}, f32[16,256]{1,0:T(8,128)S(1)}, f32[16,256]{1,0:T(8,128)S(1)}, f32[16,256]{1,0:T(8,128)S(1)}, /*index=5*/f32[16,256]{1,0:T(8,128)S(1)}) custom-call(s32[1]{0:T(128)} %bitcast.1.me_ref, f32[128,256]{1,0:T(8,128)} %bitcast.19, s32[1,128]{1,0:T(1,128)} %expo_in.1, ...), custom_call_target="tpu_custom_call" | custom-call | tf_op jit(solution)/shard_map/pallas_call | solution.py:127
  2.1 14.3 %all_to_all.21 = bf16[8,16,256]{2,1,0:T(8,128)(2,1)S(1)} all-to-all(bf16[8,16,256]{2,1,0:T(8,128)(2,1)S(1)} %bitcast.14), channel_id=1, replica_groups=mesh['zl'=4,'c'=2,'x'=4,'zh'=2,'y'=8] {'zl','c'}, dimensions={0} | all-to-all | bytes 131072 | tf_op jit(solution)/shard_map/all_to_all | solution.py:244
  16.4 0.2 clamp_convert_fusion
  16.7 25.8 %all_to_all.22 = bf16[32,16,256]{2,1,0:T(8,128)(2,1)S(1)} all-to-all(bf16[32,16,256]{2,1,0:T(8,128)(2,1)S(1)} %broadcast_in_dim.26), channel_id=1, replica_groups={{0,2,4,6,161,163,165,167,256,258,260,262,417,419,421,423,8,10,12,14,169..., dimensions={0} | all-to-all | bytes 524288 | tf_op jit(solution)/shard_map/all_to_all | solution.py:230
  42.5 0.1 broadcast_in_dim.28
  42.6 23.5 %all_to_all.23 = bf16[8,512,256]{2,1,0:T(8,128)(2,1)S(1)} all-to-all(bf16[8,512,256]{2,1,0:T(8,128)(2,1)S(1)} %broadcast_in_dim.28), channel_id=1, replica_groups={{256,257,129,128,272,273,145,144},{8,9,385,384,24,25,401,400},{264,265,..., dimensions={0} | all-to-all | bytes 4194304 | tf_op jit(solution)/shard_map/all_to_all | solution.py:230
  66.2 0.1 slice.18
  66.2 2.3 %collective-permute-start = (bf16[5,8,4,16,256]{4,3,2,1,0:T(8,128)(2,1)S(1)}, bf16[5,8,4,16,256]{4,3,2,1,0:T(8,128)(2,1)S(1)}, u32[]{:S(2)}, u32[]{:S(2)}) collective-permute-start(bf16[5,8,4,16,256]{4,3,2,1,0:T(8,128)(2,1)S(1)} %bitcast.16), channel_id=1, source_target_pairs={{0,64},{64,0},{1,65},{65,1},{2,66},{66,2},{3,67},{67,3},{4,68},{68... | collective-permute-start | bytes 3932168 | tf_op jit(solution)/shard_map/ppermute | solution.py:253
  68.5 0.1 slice.19
  68.6 2.0 %collective-permute-start.1 = (bf16[3,8,4,16,256]{4,3,2,1,0:T(8,128)(2,1)S(1)}, bf16[3,8,4,16,256]{4,3,2,1,0:T(8,128)(2,1)S(1)}, u32[]{:S(2)}, u32[]{:S(2)}) collective-permute-start(bf16[3,8,4,16,256]{4,3,2,1,0:T(8,128)(2,1)S(1)} %bitcast.18), channel_id=1, source_target_pairs={{0,64},{64,0},{1,65},{65,1},{2,66},{66,2},{3,67},{67,3},{4,68},{68... | collective-permute-start | bytes 2359304 | tf_op jit(solution)/shard_map/ppermute | solution.py:253
  70.6 0.5 collective-permute-done.other_ref.early_ref
  71.2 1.5 %shard_map.95 = (bf16[2,2,2,4,2,4,2,16,256]{8,7,6,5,4,3,2,1,0:T(8,128)(2,1)}, f32[16,256]{1,0:T(8,128)}, f32[16,256]{1,0:T(8,128)}) custom-call(s32[1]{0:T(128)} %bitcast.core_ref, bf16[8,8,4,16,256]{4,3,2,1,0:T(8,128)(2,1)S(1)} %bitcast.12, bf16[5,8,4,16,256]{4,3,2,1,0:T(8,128)(2,1)S(1)} %collective-permute-done.other_ref.early_ref, ...), custom_call_target="tpu_custom_call" | custom-call | bytes 4194304 | tf_op jit(solution)/shard_map/pallas_call | solution.py:211
  72.7 0.1 collective-permute-done.1.late_ref
  72.8 1.5 %shard_map.96 = bf16[2,2,2,4,2,4,2,16,256]{8,7,6,5,4,3,2,1,0:T(8,128)(2,1)} custom-call(s32[1]{0:T(128)} %bitcast.core_ref, bf16[8,8,4,16,256]{4,3,2,1,0:T(8,128)(2,1)S(1)} %bitcast.13, bf16[5,8,4,16,256]{4,3,2,1,0:T(8,128)(2,1)S(1)} %collective-permute-done.other_ref.early_ref, ...), custom_call_target="tpu_custom_call", output_to_operand_aliasing={{}: (4, {})} | custom-call | bytes 4194304 | tf_op jit(solution)/shard_map/pallas_call | solution.py:218
  (2 shorter events, 0.0 us)
Async XLA Ops:
  66.2 4.9 %collective-permute-start = (bf16[5,8,4,16,256]{4,3,2,1,0:T(8,128)(2,1)S(1)}, bf16[5,8,4,16,256]{4,3,2,1,0:T(8,128)(2,1)S(1)}, u32[]{:S(2)}, u32[]{:S(2)}) collective-permute-start(bf16[5,8,4,16,256]{4,3,2,1,0:T(8,128)(2,1)S(1)} %bitcast.16), channel_id=1, source_target_pairs={{0,64},{64,0},{1,65},{65,1},{2,66},{66,2},{3,67},{67,3},{4,68},{68... | collective-permute-start | bytes 3932168 | tf_op jit(solution)/shard_map/ppermute | solution.py:253
  68.6 4.2 %collective-permute-start.1 = (bf16[3,8,4,16,256]{4,3,2,1,0:T(8,128)(2,1)S(1)}, bf16[3,8,4,16,256]{4,3,2,1,0:T(8,128)(2,1)S(1)}, u32[]{:S(2)}, u32[]{:S(2)}) collective-permute-start(bf16[3,8,4,16,256]{4,3,2,1,0:T(8,128)(2,1)S(1)} %bitcast.18), channel_id=1, source_target_pairs={{0,64},{64,0},{1,65},{65,1},{2,66},{66,2},{3,67},{67,3},{4,68},{68... | collective-permute-start | bytes 2359304 | tf_op jit(solution)/shard_map/ppermute | solution.py:253
